TPU v7x, 512 devices: a whole 4x8x8 slice. The times are simulated.
512 devices in a mesh: rows: 64 (over z, y), cols: 8 (over x, core).
Axes of the slice: x: 4, y: 8, z: 8, core: 2. Of those that a mesh axis runs over, the one named last changes fastest.
Arguments:
- archive: float32 [98304, 4096], P('rows', 'cols'), may hold values from -6 to 6
- sketch: float32 [4096, 512], P('cols'), may hold values from -0.09375 to 0.09375
Outputs:
- scaled_basis: float32 [98304, 512], P(('rows', 'cols'))
- projected: float32 [4096, 512], P(('cols', 'rows'))
All inputs are finite; a program needn't handle non-finite values.
Results may differ from a plain program's by a relative error of at most 0.0003.
Values sent between devices are 32-bit elements; how exact they have to be, the bound alone decides.
No kernel may reach another device: no remote copies, remote signals or barrier semaphores. Data moves between devices by JAX's collectives and lax.ppermute only.
A program may use at most 64 MiB of HBM per device.

v0:
```python
import math

import jax
import jax.numpy as jnp
from jax import lax
from jax.sharding import PartitionSpec as P


def right_solve(factor, matrix):
    return lax.linalg.triangular_solve(
        factor, matrix, left_side=False, lower=True, transpose_a=True
    )


def local(archive, sketch):
    precise = lax.Precision.HIGHEST
    rows_here = archive.shape[0]
    slice_rows = rows_here // lax.axis_size("cols")
    col_position = lax.axis_index("cols")
    full_images = lax.psum(
        jnp.dot(archive, sketch, precision=precise, preferred_element_type=jnp.float32), "cols"
    )
    own_images = lax.dynamic_slice_in_dim(full_images, col_position * slice_rows, slice_rows, 0)
    summed = lax.psum(
        lax.dot_general(
            full_images,
            full_images,
            (((0,), (0,)), ((), ())),
            precision=precise,
            preferred_element_type=jnp.float32,
        ),
        "rows",
    )
    factor = jnp.linalg.cholesky(summed)
    basis_out = right_solve(factor, own_images)
    full_basis = right_solve(factor, full_images)
    projected = lax.psum_scatter(
        lax.dot_general(
            archive,
            full_basis,
            (((0,), (0,)), ((), ())),
            precision=precise,
            preferred_element_type=jnp.float32,
        ),
        "rows",
        scatter_dimension=0,
        tiled=True,
    )
    scale_factor = math.sqrt(rows_here * lax.axis_size("rows"))
    return (basis_out * scale_factor, projected)


def solution(mesh):
    placed = (P("rows", "cols"), P("cols", None))
    return jax.shard_map(
        local,
        mesh=mesh,
        in_specs=placed,
        out_specs=(P(("rows", "cols"), None), P(("cols", "rows"), None)),
        check_vma=False,
    )
```

profile of v0, /device:TPU:1, one launch (start us, length us, event | category | flops | bytes accessed | tf_op | source)
XLA Modules:
  0.0 608.4 jit_solution(1177792108794129878)
XLA Ops:
  7.2 1.8 copy-done
  9.1 7.5 %fusion.62 = f32[1536,512]{1,0:T(8,128)} fusion(f32[1536,512]{1,0:T(8,128)S(1)} %copy-done, f32[512,512]{1,0:T(8,128)} %param.3), kind=kOutput, calls=%fused_computation.100 | convolution fusion | flops 4831838208 | bytes 7340032 | tf_op jit(solution)/shard_map/dot_general | solution.py:21
  16.7 83.5 %all-reduce.6.cloned.1.call-done = f32[1536,512]{1,0:T(8,128)} async-done(((f32[1536,512]{1,0:T(8,128)}), f32[1536,512]{1,0:T(8,128)}) %all-reduce.6.cloned.1.call-update) | async-done | bytes 3145744 | tf_op jit(solution)/shard_map/psum | solution.py:20
  100.2 9.1 %fusion.63 = f32[512,512]{0,1:T(8,128)} fusion(f32[1536,512]{1,0:T(8,128)} %all-reduce.6.cloned.1.call-done), kind=kOutput, calls=%fused_computation.101 | convolution fusion | flops 4831838208 | bytes 4194304 | tf_op jit(solution)/shard_map/dot_general | solution.py:25
  109.5 1.3 dynamic-slice.3
  111.5 155.8 %all-reduce.8.cloned.1.call-done = f32[512,512]{0,1:T(8,128)} async-done(((f32[512,512]{0,1:T(8,128)}), f32[512,512]{0,1:T(8,128)}) %all-reduce.8.cloned.1.call-update) | async-done | bytes 1048592 | tf_op jit(solution)/shard_map/psum | solution.py:24
  267.3 2.5 copy.8
  269.8 1.8 fusion.19
  272.6 11.7 %cholesky.104 = f32[128,128]{1,0:T(8,128)S(1)} custom-call(f32[128,128]{1,0:T(8,128)S(1)} %cholesky.266), custom_call_target="Cholesky" | custom-call | tf_op jit(solution)/shard_map/jit(cholesky)/cholesky | solution.py:34
  285.4 9.8 %custom-call.32 = f32[1,128,128]{1,2,0:T(8,128)S(1)} custom-call(f32[1,128,128]{2,1,0:T(8,128)S(1)} %get-tuple-element.33), custom_call_target="InvertDiagBlocksLowerTriangular" | custom-call | tf_op jit(solution)/shard_map/jit(cholesky)/cholesky | solution.py:34
  295.2 1.9 constant_dynamic-update-slice_fusion.3
  298.5 11.7 %cholesky.217 = f32[128,128]{1,0:T(8,128)S(1)} custom-call(f32[128,128]{1,0:T(8,128)S(1)} %cholesky.270), custom_call_target="Cholesky" | custom-call | tf_op jit(solution)/shard_map/jit(cholesky)/cholesky | solution.py:34
  310.8 10.2 %custom-call.33 = f32[1,128,128]{1,2,0:T(8,128)S(1)} custom-call(f32[1,128,128]{2,1,0:T(8,128)S(1)} %get-tuple-element.30), custom_call_target="InvertDiagBlocksLowerTriangular" | custom-call | tf_op jit(solution)/shard_map/jit(cholesky)/cholesky | solution.py:34
  321.9 1.4 convolution_subtract_fusion.4
  323.4 11.7 %cholesky.238 = f32[128,128]{1,0:T(8,128)S(1)} custom-call(f32[128,128]{1,0:T(8,128)S(1)} %cholesky.275), custom_call_target="Cholesky" | custom-call | tf_op jit(solution)/shard_map/jit(cholesky)/cholesky | solution.py:34
  335.7 9.8 %custom-call.34 = f32[1,128,128]{1,2,0:T(8,128)S(1)} custom-call(f32[1,128,128]{2,1,0:T(8,128)S(1)} %get-tuple-element.27), custom_call_target="InvertDiagBlocksLowerTriangular" | custom-call | tf_op jit(solution)/shard_map/jit(cholesky)/cholesky | solution.py:34
  346.4 1.4 convolution_subtract_fusion.8
  347.8 11.7 %cholesky.255 = f32[128,128]{1,0:T(8,128)S(1)} custom-call(f32[128,128]{1,0:T(8,128)S(1)} %convolution_subtract_fusion.8), custom_call_target="Cholesky" | custom-call | tf_op jit(solution)/shard_map/jit(cholesky)/cholesky | solution.py:34
  364.5 2.5 select_select_fusion
  367.0 13.8 %while.1 = (s32[]{:T(128)}, f32[512,512]{1,0:T(8,128)}, s32[4,2]{0,1:T(2,128)S(1)}, f32[4,128,128]{2,1,0:T(8,128)}, s32[]{:T(128)}) while((s32[]{:T(128)}, f32[512,512]{1,0:T(8,128)}, s32[4,2]{0,1:T(2,128)S(1)}, f32[4,128,128]{2,1,0:T(8,128)}, s32[]{:T(128)}) %tuple.33), condition=%wide.while_cond, body=%wide.while_body.sunk | while | flops 2 | bytes 132205 | solution.py:10
  367.7 2.9 bitcast_dynamic-update-slice_fusion.2
  371.1 2.9 bitcast_dynamic-update-slice_fusion.2
  374.6 2.9 bitcast_dynamic-update-slice_fusion.2
  378.1 2.8 bitcast_dynamic-update-slice_fusion.2
  380.9 40.1 %custom-call.35 = f32[4,128,128]{1,2,0:T(8,128)S(1)} custom-call(f32[4,128,128]{2,1,0:T(8,128)} %get-tuple-element.9), custom_call_target="InvertDiagBlocksLowerTriangular" | custom-call | tf_op jit(solution)/shard_map/triangular_solve | solution.py:10
  421.0 2.1 fusion.20
  423.2 2.6 convolution_subtract_fusion.2
  426.6 3.5 convolution_subtract_fusion
  431.0 5.0 convolution_subtract_fusion.1
  436.9 6.4 %fusion.16 = f32[512,512]{0,1:T(8,128)} fusion(f32[1536,512]{1,0:T(8,128)S(1)} %copy-done, f32[1536,128]{0,1:T(8,128)S(1)} %fusion.51, f32[1536,128]{0,1:T(8,128)S(1)} %fusion.49, f32[1536,128]{0,1:T(8,128)S(1)} %fusion.47, f32[1536,128]{0,1:T(8,128)S(1)} %fusion.20), kind=kOutput, calls=%fused_computation.21 | convolution fusion | flops 4834197504 | bytes 7340032 | tf_op jit(solution)/shard_map/dot_general | solution.py:38
  447.4 1.4 convolution_subtract_fusion.6
  449.9 149.9 %all-reduce.10.cloned.1.call-done = f32[512,512]{0,1:T(8,128)} async-done(((f32[512,512]{0,1:T(8,128)}), f32[512,512]{0,1:T(8,128)}) %all-reduce.10.cloned.1.call-update) | async-done | bytes 1048592
  (48 shorter events, 21.4 us)
Async XLA Ops:
  7.2 1.9 copy-start
  7.2 93.0 %all-reduce.6.cloned.1.call-start = ((), (), s32[]{:S(2)}) async-start(), calls=%async_computation | async-start | bytes 6291456 | tf_op jit(solution)/shard_map/psum | solution.py:20
  16.6 250.6 %all-reduce.8.cloned.1.call-start = ((), (), s32[]{:S(2)}) async-start(), calls=%async_computation.1 | async-start | bytes 2097152 | tf_op jit(solution)/shard_map/psum | solution.py:24
  109.3 490.5 %all-reduce.10.cloned.1.call-start = ((), (), s32[]{:S(2)}) async-start(), calls=%async_computation.2 | async-start | bytes 2097152
  271.6 1.0 copy-start.2
  421.0 5.6 copy-start.1
Sparse Core Ops, SparseCore 0:
  16.7 83.3 all-reduce.5
  109.4 157.8 all-reduce.7
  443.4 156.3 all-reduce.9
where the time goes:
time: 617 us; the launch traced here: 608 us
  waiting for transfers between devices  389 us (63%)
  other arithmetic  126 us (20%)
  matrix products  52.4 us (8%)
  local copies, waits for them, and re-layouts  23.4 us (4%)
  between operations  17.3 us (3%)
    psum x1, waiting for transfers between devices, local(): lax.psum(lax.dot_general(full_images, full_images, (((0,), (0,)), ((), ()...  156 us
    unnamed x4, waiting for transfers between devices  150 us
    psum x1, waiting for transfers between devices, local(): lax.psum(jnp.dot(archive, sketch, precision=precise, preferred_element_ty...  83.5 us
    another operation x14, other arithmetic, local(): factor = jnp.linalg.cholesky(summed)  80.5 us
    another operation x3, other arithmetic, right_solve(): lax.linalg.triangular_solve(factor, matrix, left_side=False, lower=True,...  42.6 us
    another operation x14, matrix products, right_solve(): lax.linalg.triangular_solve(factor, matrix, left_side=False, lower=True,...  21.6 us
    another operation x12, local copies, waits for them, and re-layouts  13.8 us
  transfers between devices with their start and end apart: 3, of which 3 were waited for; matrix products, arithmetic and copies ran while one was open for 1% of the time, Pallas kernels for 0%

commit v1 on v0

v1 whole, which is shorter than its diff:
```python
import functools
import math

import jax
import jax.numpy as jnp
from jax import lax
from jax.experimental import pallas as pl
from jax.experimental.pallas import tpu as pltpu
from jax.sharding import Mesh
from jax.sharding import PartitionSpec as P

CORES = 2
BLOCK = 128
F32 = jnp.float32
BF16 = jnp.bfloat16
HIGHEST = lax.Precision.HIGHEST
VMEM = 48 * 2**20


def exact_dot(a, b, contract):
    return lax.dot_general(
        a, b, (contract, ((), ())), precision=HIGHEST, preferred_element_type=F32
    )


def halves(a):
    high = a.astype(BF16)
    return high, (a - high.astype(F32)).astype(BF16)


def three_pass_dot(a, b, contract):
    (a_high, a_low), (b_high, b_low) = a, b
    dot = functools.partial(
        lax.dot_general,
        dimension_numbers=(contract, ((), ())),
        preferred_element_type=F32,
    )
    return dot(a_high, b_high) + (dot(a_high, b_low) + dot(a_low, b_high))


def images_kernel(archive_ref, sketch_ref, out_ref, high_ref, low_ref):
    @pl.when(pl.program_id(0) == 0)
    def _():
        high_ref[...], low_ref[...] = halves(sketch_ref[...])

    out_ref[...] = three_pass_dot(
        halves(archive_ref[...]), (high_ref[...], low_ref[...]), ((1,), (0,))
    )


def partial_images(archive, sketch, groups):
    rows, depth = archive.shape
    width = sketch.shape[1]
    block = rows // (groups * CORES)
    return pl.pallas_call(
        images_kernel,
        grid=(groups * CORES,),
        in_specs=[
            pl.BlockSpec((block, depth), lambda i: (i % groups * CORES + i // groups, 0)),
            pl.BlockSpec((depth, width), lambda i: (0, 0)),
        ],
        out_specs=pl.BlockSpec((block, width), lambda i: (i, 0)),
        out_shape=jax.ShapeDtypeStruct((rows, width), F32),
        scratch_shapes=[pltpu.VMEM((depth, width), BF16)] * 2,
        compiler_params=pltpu.CompilerParams(vmem_limit_bytes=VMEM),
        cost_estimate=pl.CostEstimate(
            flops=6 * rows * depth * width, bytes_accessed=8 * rows * depth, transcendentals=0
        ),
    )(archive, sketch)


def products_kernel(slab_rows, place_ref, archive_ref, images_ref, gram_ref, moved_ref, slab_ref):
    step = pl.program_id(0)
    first = pl.multiple_of(place_ref[0] * BLOCK, BLOCK)

    @pl.when(step == 0)
    def _():
        moved_ref[...] = jnp.zeros_like(moved_ref)
        slab_ref[...] = jnp.zeros_like(slab_ref)

    images = halves(images_ref[...])
    moved_ref[...] += three_pass_dot(halves(archive_ref[...]), images, ((0,), (0,)))
    slab_ref[...] += three_pass_dot(halves(images_ref[:, pl.ds(first, BLOCK)]), images, ((0,), (0,)))

    @pl.when(step == pl.num_programs(0) - 1)
    def _():
        inside = pl.multiple_of(place_ref[1] * slab_rows, slab_rows)
        gram_ref[...] = slab_ref[pl.ds(inside, slab_rows), :]


def products(archive, images, position, groups, slab_rows):
    rows, depth = archive.shape
    width = images.shape[1]
    block = rows // (groups * CORES)
    slabs = BLOCK // slab_rows
    place = jnp.stack([position // slabs, position % slabs]).astype(jnp.int32)
    return pl.pallas_call(
        functools.partial(products_kernel, slab_rows),
        grid_spec=pltpu.PrefetchScalarGridSpec(
            num_scalar_prefetch=1,
            grid=(groups * CORES,),
            in_specs=[
                pl.BlockSpec((block, depth), lambda i, place: (i % groups * CORES + i // groups, 0)),
                pl.BlockSpec((block, width), lambda i, place: (i, 0)),
            ],
            out_specs=[
                pl.BlockSpec((slab_rows, width), lambda i, place: (0, 0)),
                pl.BlockSpec((depth, width), lambda i, place: (0, 0)),
            ],
            scratch_shapes=[pltpu.VMEM((BLOCK, width), F32)],
        ),
        out_shape=[
            jax.ShapeDtypeStruct((slab_rows, width), F32),
            jax.ShapeDtypeStruct((depth, width), F32),
        ],
        compiler_params=pltpu.CompilerParams(vmem_limit_bytes=VMEM),
        cost_estimate=pl.CostEstimate(
            flops=8 * rows * depth * width, bytes_accessed=8 * rows * depth, transcendentals=0
        ),
    )(place, archive, images)


def factor_block(rows):
    shape = rows[0].shape
    lane = lax.broadcasted_iota(jnp.int32, shape, 1)
    sub = lax.broadcasted_iota(jnp.int32, shape, 0)
    count = len(rows)
    result = []

    def column(slab, at):
        return jnp.broadcast_to(slab[:, at : at + 1], shape)

    def row(slab, at):
        return jnp.broadcast_to(slab[at : at + 1, :], shape)

    for p in range(count):
        panel = rows[p]
        columns = [column(panel, 8 * p + j) for j in range(8)]
        kept = jnp.zeros(shape, F32)
        roots = jnp.zeros(shape, F32)
        for j in range(8):
            here = lane == 8 * p + j
            at = sub == j
            pivot = row(columns[j], j)
            inverse = 1.0 / pivot
            current = jnp.where(here, 1.0, row(panel, j))
            kept = jnp.where(at, current, kept)
            roots = jnp.where(at, lax.rsqrt(pivot), roots)
            scaled = current * inverse
            panel = jnp.where(at, scaled, jnp.where(here, 0.0, panel) - columns[j] * scaled)
            for k in range(j + 1, 8):
                part = row(columns[k], j) * inverse
                columns[k] = jnp.where(at, part, columns[k] - columns[j] * part)
        result.append(jnp.where(lane <= sub + 8 * p, kept * roots, 0.0))
        own = (lane >= 8 * p) & (lane < 8 * p + 8)
        spread = [row(panel, j) for j in range(8)]
        for i in range(p + 1, count):
            terms = [column(rows[i], 8 * p + j) * spread[j] for j in range(8)]
            while len(terms) > 1:
                terms = [terms[a] + terms[a + 1] for a in range(0, len(terms), 2)]
            rows[i] = jnp.where(own, 0.0, rows[i]) - terms[0]
    return result


def factor_kernel(scale, gram_ref, images_ref, inverse_ref, basis_ref, work_ref, small_ref, panel_ref):
    size = gram_ref.shape[0]
    blocks = size // BLOCK
    work_ref[...] = gram_ref[...]
    column = lax.broadcasted_iota(jnp.int32, (BLOCK, size), 1)
    unit = (
        lax.broadcasted_iota(jnp.int32, (BLOCK, BLOCK), 0)
        == lax.broadcasted_iota(jnp.int32, (BLOCK, BLOCK), 1)
    ).astype(F32)

    def block_step(k, carry):
        first = pl.multiple_of(k * BLOCK, BLOCK)
        here = pl.ds(first, BLOCK)
        slabs = factor_block([work_ref[pl.ds(first + 8 * i, 8), here] for i in range(BLOCK // 8)])
        for i, slab in enumerate(slabs):
            small_ref[8 * i : 8 * i + 8, :] = slab
        work_ref[here, here] = unit
        panel = exact_dot(small_ref[...], work_ref[here, :], ((1,), (0,)))
        panel_ref[...] = panel
        finished = jnp.where(column < first + BLOCK, panel, 0.0)
        inverse_ref[here, :] = finished
        own = (column >= first) & (column < first + BLOCK)

        def update(i, inner):
            there = pl.ds(pl.multiple_of(i * BLOCK, BLOCK), BLOCK)
            kept = jnp.where(own, 0.0, work_ref[there, :])
            work_ref[there, :] = kept - exact_dot(panel_ref[:, there], panel_ref[...], ((0,), (0,)))
            return inner

        lax.fori_loop(k + 1, blocks, update, 0)
        basis_ref[:, here] = scale * exact_dot(images_ref[...], finished, ((1,), (1,)))
        return carry

    lax.fori_loop(0, blocks, block_step, 0)


def factor(gram, images, scale):
    size = gram.shape[0]
    return pl.pallas_call(
        functools.partial(factor_kernel, scale),
        in_specs=[pl.BlockSpec(memory_space=pltpu.VMEM)] * 2,
        out_specs=[pl.BlockSpec(memory_space=pltpu.VMEM)] * 2,
        out_shape=[
            jax.ShapeDtypeStruct(gram.shape, F32),
            jax.ShapeDtypeStruct(images.shape, F32),
        ],
        scratch_shapes=[
            pltpu.VMEM((size, size), F32),
            pltpu.VMEM((BLOCK, BLOCK), F32),
            pltpu.VMEM((BLOCK, size), F32),
        ],
        compiler_params=pltpu.CompilerParams(vmem_limit_bytes=VMEM),
        cost_estimate=pl.CostEstimate(
            flops=40 * size**3, bytes_accessed=12 * size**2, transcendentals=2 * size
        ),
    )(gram, images)


def exchange(blocks, axes):
    return lax.all_to_all(blocks, axes, 0, 0, tiled=True)


def gather(block, axes):
    size = lax.axis_size(axes)
    return exchange(jnp.broadcast_to(block[None], (size, *block.shape)), axes)


def local(archive, sketch):
    groups = lax.axis_size("x")
    over_rows = ("z", "y")
    stacked = lax.axis_size("z") * lax.axis_size("y")
    rows_here = archive.shape[0]
    width = sketch.shape[1]
    own_rows = rows_here // (groups * CORES)
    slab_rows = width // (groups * CORES)
    scale = math.sqrt(rows_here * stacked)

    partial = partial_images(archive, sketch, groups)
    by_core = exchange(partial.reshape(CORES, groups * own_rows, width), "core").sum(0)
    own_images = exchange(by_core.reshape(groups, own_rows, width), "x").sum(0)
    core_images = gather(own_images, "x").reshape(groups * own_rows, width)
    images = gather(core_images, "core").reshape(rows_here, width)

    position = lax.axis_index("core") * groups + lax.axis_index("x")
    gram, moved = products(archive, images, position, groups, slab_rows)

    moved = lax.psum_scatter(moved, "z", scatter_dimension=0, tiled=True)
    moved = lax.psum_scatter(moved, "y", scatter_dimension=0, tiled=True)

    pieces = gram.reshape(stacked, -1, BLOCK)
    gram = gather(exchange(pieces, over_rows).reshape(stacked, *pieces.shape[1:]).sum(0), over_rows)
    gram = gather(gather(gram.reshape(slab_rows, width), "x").reshape(groups * slab_rows, width), "core")
    inverse, basis = factor(gram.reshape(width, width), own_images, scale)
    return basis, exact_dot(moved, inverse, ((1,), (1,)))


def solution(mesh):
    rows, cols = mesh.devices.shape
    across = math.isqrt(rows)
    fine = Mesh(
        mesh.devices.reshape(rows // across, across, cols // CORES, CORES), ("z", "y", "x", "core")
    )
    return jax.shard_map(
        local,
        mesh=fine,
        in_specs=(P(("z", "y"), ("x", "core")), P(("x", "core"), None)),
        out_specs=(P(("z", "y", "x", "core"), None), P(("x", "core", "z", "y"), None)),
        check_vma=False,
    )
```

time: 617 us -> 194 us (0.31)
  the two profiles are of different devices: /device:TPU:1 before, /device:TPU:4 now
where the time goes in v1:
time: 194 us; the launch traced here: 193 us
  blocking collectives  92.8 us (48%)
  Pallas kernels  41.8 us (22%)
  waiting for transfers between devices  26.3 us (14%)
  between operations  14.1 us (7%)
  starting transfers between devices  9.86 us (5%)
  local copies, waits for them, and re-layouts  4.26 us (2%)
  matrix products  2.29 us (1%)
    all_to_all x6, blocking collectives, exchange(): return lax.all_to_all(blocks, axes, 0, 0, tiled=True)  92.8 us
    pallas_call x1, Pallas kernels, factor(): pl.pallas_call(functools.partial(factor_kernel, scale), in_specs=[pl.Bloc...  25.8 us
    all_to_all x2, waiting for transfers between devices, exchange(): return lax.all_to_all(blocks, axes, 0, 0, tiled=True)  18.8 us
    all_to_all x2, starting transfers between devices, exchange(): return lax.all_to_all(blocks, axes, 0, 0, tiled=True)  9.82 us
    pallas_call x1, Pallas kernels, products(): pl.pallas_call(functools.partial(products_kernel, slab_rows), grid_spec=p...  9.33 us
    reduce_scatter x1, waiting for transfers between devices, local(): moved = lax.psum_scatter(moved, 'y', scatter_dimension=0, tiled=True)  6.87 us
    pallas_call x1, Pallas kernels, partial_images(): pl.pallas_call(images_kernel, grid=(groups * CORES,), in_specs=[pl.BlockS...  6.71 us
  transfers between devices with their start and end apart: 4, of which 3 were waited for; matrix products, arithmetic and copies ran while one was open for 1% of the time, Pallas kernels for 13%

profile of v1, /device:TPU:4, one launch (start us, length us, event | category | flops | bytes accessed | tf_op | source)
XLA Modules:
  0.0 193.3 jit_solution(8892911125532641409)
XLA Ops:
  7.2 0.0 copy-start.1
  7.2 1.2 copy-done.1
  8.4 6.7 %shard_map.41 = f32[1536,512]{1,0:T(8,128)S(1)} custom-call(f32[1536,512]{1,0:T(8,128)} %archive_ref.3, f32[512,512]{1,0:T(8,128)S(1)} %copy-done.1), custom_call_target="tpu_custom_call" | custom-call | flops 2415919104 | bytes 6291456 | tf_op jit(solution)/shard_map/pallas_call | solution.py:55
  15.1 6.3 %all_to_all.40 = f32[2,768,512]{2,1,0:T(8,128)S(1)} all-to-all(f32[2,768,512]{2,1,0:T(8,128)S(1)} %bitcast.14), channel_id=1, replica_groups=mesh['z'=8,'y'=8,'x'=4,'core'=2] {'core'}, dimensions={0} | all-to-all | bytes 6291456 | tf_op jit(solution)/shard_map/all_to_all | solution.py:224
  21.4 1.6 reduce_sum.27
  22.9 28.0 %all_to_all.41 = f32[4,192,512]{2,1,0:T(8,128)S(1)} all-to-all(f32[4,192,512]{2,1,0:T(8,128)} %bitcast.16), channel_id=1, replica_groups=mesh['z'=8,'y'=8,'x'=4,'core'=2] {'x'}, dimensions={0} | all-to-all | bytes 3145728 | tf_op jit(solution)/shard_map/all_to_all | solution.py:224
  50.9 0.2 reduce_sum.28.images_ref
  51.1 1.4 broadcast_in_dim.16
  52.4 6.2 %all-to-all-start.2 = ((f32[4,192,512]{2,1,0:T(8,128)}), f32[4,192,512]{2,1,0:T(8,128)S(1)}, u32[]{:S(2)}, u32[]{:S(2)}) async-start(f32[4,192,512]{2,1,0:T(8,128)} %broadcast_in_dim.16), calls=%async_computation.2 | async-start | bytes 3145728 | tf_op jit(solution)/shard_map/all_to_all | solution.py:224
  58.7 0.0 reduce-scatter.3.cloned.1.call-start
  58.7 0.1 pad_add_fusion.place_ref
  58.8 17.4 %all-to-all-done.2 = f32[4,192,512]{2,1,0:T(8,128)S(1)} async-done(((f32[4,192,512]{2,1,0:T(8,128)}), f32[4,192,512]{2,1,0:T(8,128)S(1)}, u32[]{:S(2)}, u32[]{:S(2)}) %all-to-all-start.2) | async-done | bytes 1572896 | tf_op jit(solution)/shard_map/all_to_all | solution.py:224
  76.2 0.4 broadcast_in_dim.35
  76.6 0.0 copy-start
  76.6 7.5 %all_to_all.42 = f32[2,768,512]{2,1,0:T(8,128)} all-to-all(f32[2,768,512]{2,1,0:T(8,128)S(1)} %broadcast_in_dim.35), channel_id=1, replica_groups=mesh['z'=8,'y'=8,'x'=4,'core'=2] {'core'}, dimensions={0} | all-to-all | bytes 6291456 | tf_op jit(solution)/shard_map/all_to_all | solution.py:224
  84.1 0.0 copy-done
  84.1 9.3 %shard_map.42 = (f32[64,512]{1,0:T(8,128)S(1)}, f32[512,512]{1,0:T(8,128)}) custom-call(s32[2]{0:T(128)S(1)} %pad_add_fusion.place_ref, f32[1536,512]{1,0:T(8,128)S(1)} %copy-done, f32[1536,512]{1,0:T(8,128)} %bitcast.18), custom_call_target="tpu_custom_call" | custom-call | flops 3221225472 | bytes 6291456 | tf_op jit(solution)/shard_map/pallas_call | solution.py:97
  93.5 0.0 reduce-scatter.3.cloned.1.call-update
  93.5 23.8 %all_to_all.43 = f32[64,4,128]{2,1,0:T(4,128)S(1)} all-to-all(f32[64,4,128]{2,1,0:T(4,128)S(1)} %reshape.27), channel_id=1, replica_groups=mesh['z'=8,'y'=8,'x'=4,'core'=2] {'z','y'}, dimensions={0} | all-to-all | bytes 262144 | tf_op jit(solution)/shard_map/all_to_all | solution.py:224
  117.3 0.1 reduce_sum.29
  117.4 16.6 %all_to_all.44 = f32[64,4,128]{2,1,0:T(4,128)S(1)} all-to-all(f32[64,4,128]{2,1,0:T(4,128)S(1)} %broadcast_in_dim.36), channel_id=1, replica_groups=mesh['z'=8,'y'=8,'x'=4,'core'=2] {'z','y'}, dimensions={0} | all-to-all | bytes 262144 | tf_op jit(solution)/shard_map/all_to_all | solution.py:224
  134.0 0.1 broadcast_in_dim.38
  134.0 10.7 %all_to_all.45 = f32[4,64,512]{2,1,0:T(8,128)S(1)} all-to-all(f32[4,64,512]{2,1,0:T(8,128)S(1)} %broadcast_in_dim.38), channel_id=1, replica_groups=mesh['z'=8,'y'=8,'x'=4,'core'=2] {'x'}, dimensions={0} | all-to-all | bytes 1048576 | tf_op jit(solution)/shard_map/all_to_all | solution.py:224
  144.8 1.1 broadcast_in_dim.40
  145.9 3.6 %all-to-all-start.7 = ((f32[2,256,512]{2,1,0:T(8,128)}), f32[2,256,512]{2,1,0:T(8,128)S(1)}, u32[]{:S(2)}, u32[]{:S(2)}) async-start(f32[2,256,512]{2,1,0:T(8,128)} %broadcast_in_dim.40), calls=%async_computation.7 | async-start | bytes 2097152 | tf_op jit(solution)/shard_map/all_to_all | solution.py:224
  149.5 0.0 reduce-scatter.5.cloned.1.call-start
  149.5 0.0 reduce-scatter.3.cloned.1.call-done
  149.6 0.7 reduce-scatter.5.cloned.1.call-update
  150.2 1.3 all-to-all-done.7
  151.6 25.8 %shard_map.43 = (f32[512,512]{1,0:T(8,128)S(1)}, f32[192,512]{1,0:T(8,128)}) custom-call(f32[512,512]{1,0:T(8,128)S(1)} %bitcast.15, f32[192,512]{1,0:T(8,128)S(1)} %reduce_sum.28.images_ref), custom_call_target="tpu_custom_call" | custom-call | flops 5368709120 | bytes 3145728 | tf_op jit(solution)/shard_map/pallas_call | solution.py:203
  177.3 6.9 %reduce-scatter.5.cloned.1.call-done = f32[8,512]{1,0:T(8,128)} async-done(((f32[64,512]{1,0:T(8,128)}), f32[8,512]{1,0:T(8,128)}) %reduce-scatter.5.cloned.1.call-update) | async-done | bytes 16400 | tf_op jit(solution)/shard_map/reduce_scatter | solution.py:252
  184.2 2.3 %fusion = f32[8,512]{1,0:T(8,128)} fusion(f32[8,512]{1,0:T(8,128)} %reduce-scatter.5.cloned.1.call-done, f32[512,512]{1,0:T(8,128)S(1)} %get-tuple-element.9), kind=kOutput, calls=%fused_computation.2 | convolution fusion | flops 25165824 | bytes 1081344 | tf_op jit(solution)/shard_map/dot_general | solution.py:21
  (3 shorter events, 0.1 us)
Async XLA Ops:
  7.2 1.2 copy-start.1
  52.4 23.7 %all-to-all-start.2 = ((f32[4,192,512]{2,1,0:T(8,128)}), f32[4,192,512]{2,1,0:T(8,128)S(1)}, u32[]{:S(2)}, u32[]{:S(2)}) async-start(f32[4,192,512]{2,1,0:T(8,128)} %broadcast_in_dim.16), calls=%async_computation.2 | async-start | bytes 3145728 | tf_op jit(solution)/shard_map/all_to_all | solution.py:224
  58.7 90.9 %reduce-scatter.3.cloned.1.call-start = ((), (), s32[]{:S(2)}) async-start(), calls=%async_computation.10 | async-start | bytes 1179648 | tf_op jit(solution)/shard_map/reduce_scatter | solution.py:251
  76.6 7.5 %copy-start = (f32[1536,512]{1,0:T(8,128)S(1)}, f32[1536,512]{1,0:T(8,128)}, u32[]{:S(2)}) copy-start(f32[1536,512]{1,0:T(8,128)} %archive_ref.3) | copy-start | bytes 9437188
  145.9 5.7 %all-to-all-start.7 = ((f32[2,256,512]{2,1,0:T(8,128)}), f32[2,256,512]{2,1,0:T(8,128)S(1)}, u32[]{:S(2)}, u32[]{:S(2)}) async-start(f32[2,256,512]{2,1,0:T(8,128)} %broadcast_in_dim.40), calls=%async_computation.7 | async-start | bytes 2097152 | tf_op jit(solution)/shard_map/all_to_all | solution.py:224
  149.5 34.7 %reduce-scatter.5.cloned.1.call-start = ((), (), s32[]{:S(2)}) async-start(), calls=%async_computation.11 | async-start | bytes 147456 | tf_op jit(solution)/shard_map/reduce_scatter | solution.py:252
Sparse Core Ops, SparseCore 0:
  93.6 43.8 reduce-scatter.2
  153.1 31.0 reduce-scatter.4

commit v2 on v0

v2 whole, which is shorter than its diff:
```python
import functools
import math

import jax
import jax.numpy as jnp
from jax import lax
from jax.experimental import pallas as pl
from jax.experimental.pallas import tpu as pltpu
from jax.sharding import Mesh
from jax.sharding import PartitionSpec as P

CORES = 2
BLOCK = 128
GROUP = 4
F32 = jnp.float32
BF16 = jnp.bfloat16
HIGHEST = lax.Precision.HIGHEST
VMEM = 48 * 2**20


def exact_dot(a, b, contract):
    return lax.dot_general(
        a, b, (contract, ((), ())), precision=HIGHEST, preferred_element_type=F32
    )


def halves(a):
    high = a.astype(BF16)
    return high, (a - high.astype(F32)).astype(BF16)


def three_pass_dot(a, b, axis_a, axis_b):
    left = jnp.concatenate([part for high, low in a for part in (high, low, high)], axis_a)
    right = jnp.concatenate([part for high, low in b for part in (high, high, low)], axis_b)
    return lax.dot_general(
        left, right, (((axis_a,), (axis_b,)), ((), ())), preferred_element_type=F32
    )


def thirds(a):
    high = a.astype(BF16)
    rest = a - high.astype(F32)
    middle = rest.astype(BF16)
    return high, middle, (rest - middle.astype(F32)).astype(BF16)


def six_pass_dot(a, b, axis_a, axis_b):
    a0, a1, a2 = thirds(a)
    b0, b1, b2 = thirds(b)
    left = jnp.concatenate([a0, a0, a1, a0, a2, a1], axis_a)
    right = jnp.concatenate([b0, b1, b0, b2, b0, b1], axis_b)
    return lax.dot_general(
        left, right, (((axis_a,), (axis_b,)), ((), ())), preferred_element_type=F32
    )


def row_block(place, device, flip):
    return device * CORES + (1 - place[0] if flip else place[0])


def images_kernel(place_ref, archive_ref, sketch_ref, out_ref, sketch_halves):
    depth = sketch_ref.shape[0]

    @pl.when(pl.program_id(0) == 0)
    def _():
        high, low = halves(sketch_ref[...])
        sketch_halves[:depth] = high
        sketch_halves[depth : 2 * depth] = high
        sketch_halves[2 * depth :] = low

    high, low = halves(archive_ref[...])
    out_ref[...] = jnp.dot(
        jnp.concatenate([high, low, high], 1), sketch_halves[...], preferred_element_type=F32
    )


def partial_images(archive, sketch, place, groups, flip):
    rows, depth = archive.shape
    width = sketch.shape[1]
    block = rows // (groups * CORES)
    return pl.pallas_call(
        images_kernel,
        grid_spec=pltpu.PrefetchScalarGridSpec(
            num_scalar_prefetch=1,
            grid=(groups,),
            in_specs=[
                pl.BlockSpec((block, depth), lambda i, place: (row_block(place, i, flip), 0)),
                pl.BlockSpec((depth, width), lambda i, place: (0, 0)),
            ],
            out_specs=pl.BlockSpec((block, width), lambda i, place: (i, 0)),
            scratch_shapes=[pltpu.VMEM((3 * depth, width), BF16)],
        ),
        out_shape=jax.ShapeDtypeStruct((groups * block, width), F32),
        compiler_params=pltpu.CompilerParams(vmem_limit_bytes=VMEM),
        cost_estimate=pl.CostEstimate(
            flops=3 * rows * depth * width, bytes_accessed=8 * rows * depth, transcendentals=0
        ),
    )(place, archive, sketch)


def whole(shape):
    return pl.BlockSpec(shape, lambda i, place: (0,) * len(shape))


def gram_kernel(place_ref, images_ref, kept_ref, sent_ref):
    rows = kept_ref.shape[0]
    images = halves(images_ref[...])
    for core, out_ref in ((place_ref[0], kept_ref), (1 - place_ref[0], sent_ref)):
        columns = pl.ds(pl.multiple_of(core * rows, rows), rows)
        out_ref[...] = three_pass_dot([halves(images_ref[:, columns])], [images], 0, 0)


def gram_halves(images, place):
    rows, width = images.shape
    shape = (width // CORES, width)
    return pl.pallas_call(
        gram_kernel,
        grid_spec=pltpu.PrefetchScalarGridSpec(
            num_scalar_prefetch=1,
            grid=(1,),
            in_specs=[whole(images.shape)],
            out_specs=[whole(shape)] * CORES,
        ),
        out_shape=[jax.ShapeDtypeStruct(shape, F32)] * CORES,
        compiler_params=pltpu.CompilerParams(vmem_limit_bytes=VMEM),
        cost_estimate=pl.CostEstimate(
            flops=6 * rows * width * width, bytes_accessed=4 * rows * width, transcendentals=0
        ),
    )(place, images)


def moved_kernel(count, place_ref, *refs):
    archive = [halves(ref[...]) for ref in refs[:count]]
    images = [halves(ref[...]) for ref in refs[count : 2 * count]]
    refs[-1][...] = three_pass_dot(archive, images, 0, 0)


def moved_rows(archive, near, far, place, groups):
    rows, depth = archive.shape
    block, width = near[0].shape

    def chosen(shift, flip):
        def at(i, place):
            return row_block(place, lax.rem(place[1] - shift + groups, groups), flip), 0

        return pl.BlockSpec((block, depth), at)

    images = [*near, *far]
    return pl.pallas_call(
        functools.partial(moved_kernel, len(images)),
        grid_spec=pltpu.PrefetchScalarGridSpec(
            num_scalar_prefetch=1,
            grid=(1,),
            in_specs=[chosen(shift, flip) for flip in (False, True) for shift in range(groups)]
            + [whole(part.shape) for part in images],
            out_specs=whole((depth, width)),
        ),
        out_shape=jax.ShapeDtypeStruct((depth, width), F32),
        compiler_params=pltpu.CompilerParams(vmem_limit_bytes=VMEM),
        cost_estimate=pl.CostEstimate(
            flops=6 * rows * depth * width, bytes_accessed=8 * rows * depth, transcendentals=0
        ),
    )(place, *([archive] * len(images)), *images)


def factor_block(rows):
    shape = rows[0].shape
    lane = lax.broadcasted_iota(jnp.int32, shape, 1)
    sub = lax.broadcasted_iota(jnp.int32, shape, 0)
    count = len(rows)
    result = []

    def column(slab, at):
        return jnp.broadcast_to(slab[:, at : at + 1], shape)

    def row(slab, at):
        return jnp.broadcast_to(slab[at : at + 1, :], shape)

    for group in range(0, count, GROUP):
        end = group + GROUP
        finished = []
        for p in range(group, end):
            panel = rows[p]
            columns = [column(panel, 8 * p + j) for j in range(8)]
            kept = jnp.zeros(shape, F32)
            pivots = jnp.zeros(shape, F32)
            for j in range(8):
                here = lane == 8 * p + j
                at = sub == j
                pivot = row(columns[j], j)
                inverse = 1.0 / pivot
                current = jnp.where(here, 1.0, row(panel, j))
                kept = jnp.where(at, current, kept)
                pivots = jnp.where(at, pivot, pivots)
                scaled = current * inverse
                panel = jnp.where(at, scaled, jnp.where(here, 0.0, panel) - columns[j] * scaled)
                for k in range(j + 1, 8):
                    part = row(columns[k], j) * inverse
                    columns[k] = jnp.where(at, part, columns[k] - columns[j] * part)
            finished.append(kept * lax.rsqrt(pivots))
            own = (lane >= 8 * p) & (lane < 8 * p + 8)
            spread = [row(panel, j) for j in range(8)]
            for i in range(p + 1, end):
                terms = [column(rows[i], 8 * p + j) * spread[j] for j in range(8)]
                while len(terms) > 1:
                    terms = [terms[a] + terms[a + 1] for a in range(0, len(terms), 2)]
                rows[i] = jnp.where(own, 0.0, rows[i]) - terms[0]
        lower = [lane <= sub + 8 * p for p in range(group, end)]
        result += [jnp.where(keep, slab, 0.0) for keep, slab in zip(lower, finished)]
        if end < count:
            later = lane >= 8 * end
            panel = jnp.concatenate(
                [jnp.where(keep | later, slab, 0.0) for keep, slab in zip(lower, finished)], 0
            )
            change = six_pass_dot(panel, panel, 0, 0)
            own = (lane >= 8 * group) & (lane < 8 * end)
            for i in range(end, count):
                rows[i] = jnp.where(own, 0.0, rows[i]) - change[8 * i : 8 * i + 8]
    return result


def factor_kernel(scale, groups, place_ref, images_ref, *refs):
    gram_refs = refs[: 2 * groups]
    inverse_ref, basis_ref, work_ref, small_ref, panel_ref = refs[2 * groups :]
    size = work_ref.shape[0]
    blocks = size // BLOCK
    slab = gram_refs[0].shape[0]
    for flip in range(CORES):
        core = 1 - place_ref[0] if flip else place_ref[0]
        for shift in range(groups):
            owner = lax.rem(place_ref[1] - shift + groups, groups)
            first = pl.multiple_of((core * groups + owner) * slab, slab)
            work_ref[pl.ds(first, slab), :] = gram_refs[flip * groups + shift][...]
    column = lax.broadcasted_iota(jnp.int32, (BLOCK, size), 1)
    unit = (
        lax.broadcasted_iota(jnp.int32, (BLOCK, BLOCK), 0)
        == lax.broadcasted_iota(jnp.int32, (BLOCK, BLOCK), 1)
    ).astype(F32)

    def block_step(k, carry):
        first = pl.multiple_of(k * BLOCK, BLOCK)
        here = pl.ds(first, BLOCK)
        slabs = factor_block([work_ref[pl.ds(first + 8 * i, 8), here] for i in range(BLOCK // 8)])
        for i, rows in enumerate(slabs):
            small_ref[8 * i : 8 * i + 8, :] = rows
        work_ref[here, here] = unit
        panel = six_pass_dot(small_ref[...], work_ref[here, :], 1, 0)
        panel_ref[...] = panel
        finished = jnp.where(column < first + BLOCK, panel, 0.0)
        inverse_ref[here, :] = finished
        own = (column >= first) & (column < first + BLOCK)

        def update(i, inner):
            there = pl.ds(pl.multiple_of(i * BLOCK, BLOCK), BLOCK)
            kept = jnp.where(own, 0.0, work_ref[there, :])
            work_ref[there, :] = kept - six_pass_dot(panel_ref[:, there], panel_ref[...], 0, 0)
            return inner

        lax.fori_loop(k + 1, blocks, update, 0)
        basis_ref[:, here] = scale * six_pass_dot(images_ref[...], finished, 1, 1)
        return carry

    lax.fori_loop(0, blocks, block_step, 0)


def factor(pieces, images, place, scale):
    size = images.shape[1]

    return pl.pallas_call(
        functools.partial(factor_kernel, scale, len(pieces) // CORES),
        grid_spec=pltpu.PrefetchScalarGridSpec(
            num_scalar_prefetch=1,
            grid=(1,),
            in_specs=[whole(part.shape) for part in (images, *pieces)],
            out_specs=[whole((size, size)), whole(images.shape)],
            scratch_shapes=[
                pltpu.VMEM((size, size), F32),
                pltpu.VMEM((BLOCK, BLOCK), F32),
                pltpu.VMEM((BLOCK, size), F32),
            ],
        ),
        out_shape=[
            jax.ShapeDtypeStruct((size, size), F32),
            jax.ShapeDtypeStruct(images.shape, F32),
        ],
        compiler_params=pltpu.CompilerParams(vmem_limit_bytes=VMEM),
        cost_estimate=pl.CostEstimate(
            flops=2 * size**2, bytes_accessed=size, transcendentals=2 * size
        ),
    )(place, images, *pieces)


def exchange(blocks, axes):
    return lax.all_to_all(blocks, axes, 0, 0, tiled=True)


def gather(block, axes):
    size = lax.axis_size(axes)
    return exchange(jnp.broadcast_to(block[None], (size, *block.shape)), axes)


def shifted(block, axis, by):
    size = lax.axis_size(axis)
    return lax.ppermute(block, axis, [(i, (i + by) % size) for i in range(size)])


def local(archive, sketch):
    groups = lax.axis_size("x")
    over_rows = ("z", "y")
    stacked = lax.axis_size("z") * lax.axis_size("y")
    rows_here = archive.shape[0]
    width = sketch.shape[1]
    own_rows = rows_here // (groups * CORES)
    slab_rows = width // (groups * CORES)
    scale = math.sqrt(rows_here * stacked)
    place = jnp.stack([lax.axis_index("core"), lax.axis_index("x")]).astype(jnp.int32)

    theirs = partial_images(archive, sketch, place, groups, True)
    mine = partial_images(archive, sketch, place, groups, False)
    sums = mine + shifted(theirs, "core", 1)
    own = exchange(sums.reshape(groups, own_rows, width), "x").sum(0)

    kept, sent = gram_halves(own, place)
    gram = kept + shifted(sent, "core", 1)
    gram = exchange(gram.reshape(groups, slab_rows, width), "x").sum(0)
    split = gram.reshape(stacked, -1, BLOCK)
    split, late = lax.optimization_barrier((split, own))
    row = exchange(split, over_rows).sum(0).reshape(split.shape[1:])

    near = [late, *(shifted(late, "x", s) for s in range(1, groups))]
    row, near = lax.optimization_barrier((row, near))
    far = shifted(jnp.concatenate(near, 0), "core", 1)
    far = [far[s * own_rows : (s + 1) * own_rows] for s in range(groups)]
    moved = moved_rows(archive, near, far, place, groups)

    gram = gather(row, over_rows).reshape(slab_rows, width)
    moved = exchange(moved.reshape(stacked, -1, width), over_rows)
    here = [gram, *(shifted(gram, "x", s) for s in range(1, groups))]
    there = shifted(jnp.concatenate(here, 0), "core", 1)
    there = [there[s * slab_rows : (s + 1) * slab_rows] for s in range(groups)]
    inverse, basis = factor(here + there, own, place, scale)
    return basis, exact_dot(moved.sum(0), inverse, ((1,), (1,)))


def solution(mesh):
    rows, cols = mesh.devices.shape
    across = math.isqrt(rows)
    fine = Mesh(
        mesh.devices.reshape(rows // across, across, cols // CORES, CORES), ("z", "y", "x", "core")
    )
    return jax.shard_map(
        local,
        mesh=fine,
        in_specs=(P(("z", "y"), ("x", "core")), P(("x", "core"), None)),
        out_specs=(P(("z", "y", "x", "core"), None), P(("x", "core", "z", "y"), None)),
        check_vma=False,
    )
```

time: 617 us -> 164 us (0.27); the launches traced: 608 us -> 163 us
  waiting for transfers between devices: 389 us -> 11.4 us
  other arithmetic: 126 us -> 2.19 us
  blocking collectives: 0 us -> 58.2 us
  matrix products: 52.4 us -> 1.58 us
  starting transfers between devices: 0.3 us -> 50.5 us
  Pallas kernels: 0 us -> 34.7 us
  local copies, waits for them, and re-layouts: 23.4 us -> 4 us
  between operations: 17.3 us -> 0.83 us
    psum x2 -> x0, waiting for transfers between devices: 239 us -> none  [the longest x1 156 us: local(): lax.psum(lax.dot_general(full_images, full_images, (((0,), (0,)), ((), ()...]
    unnamed x4 -> x0, waiting for transfers between devices: 150 us -> none
    another operation x17 -> x1, other arithmetic: 123 us -> 0.08 us  [local(): jnp.stack([lax.axis_index('core'), lax.axis_index('x')]).astype(jnp.int32)]
    all_to_all x0 -> x3, blocking collectives: none -> 58.2 us  [exchange(): return lax.all_to_all(blocks, axes, 0, 0, tiled=True)]
    ppermute x0 -> x10, starting transfers between devices: none -> 39.5 us  [shifted(): lax.ppermute(block, axis, [(i, (i + by) % size) for i in range(size)])]
    pallas_call x0 -> x5, Pallas kernels: none -> 34.7 us  [the longest x1 22 us: factor(): pl.pallas_call(functools.partial(factor_kernel, scale, len(pieces) // COR...]
    another operation x20 -> x0, matrix products: 29.4 us -> none  [the longest x14 21.6 us: right_solve(): lax.linalg.triangular_solve(factor, matrix, left_side=False, lower=True,...]
    dot_general x3 -> x1, matrix products: 23 us -> 1.58 us  [exact_dot(): lax.dot_general(a, b, (contract, ((), ())), precision=HIGHEST, preferred_...]
  transfers between devices with their start and end apart: 3 -> 12, of which waited for: 3 -> 6; matrix products, arithmetic and copies ran while one was open for 1% -> 1% of each run, Pallas kernels for 0% -> 19%
where the time goes in v2:
time: 164 us; the launch traced here: 163 us
  blocking collectives  58.2 us (35%)
  starting transfers between devices  50.5 us (31%)
  Pallas kernels  34.7 us (21%)
  waiting for transfers between devices  11.4 us (7%)
  local copies, waits for them, and re-layouts  4 us (2%)
  other arithmetic  2.19 us (1%)
    all_to_all x3, blocking collectives, exchange(): return lax.all_to_all(blocks, axes, 0, 0, tiled=True)  58.2 us
    ppermute x10, starting transfers between devices, shifted(): lax.ppermute(block, axis, [(i, (i + by) % size) for i in range(size)])  39.5 us
    pallas_call x1, Pallas kernels, factor(): pl.pallas_call(functools.partial(factor_kernel, scale, len(pieces) // COR...  22 us
    all_to_all x2, starting transfers between devices, exchange(): return lax.all_to_all(blocks, axes, 0, 0, tiled=True)  11 us
    pallas_call x1, Pallas kernels, moved_rows(): pl.pallas_call(functools.partial(moved_kernel, len(images)), grid_spec=pl...  6.03 us
    all_to_all x2, waiting for transfers between devices, exchange(): return lax.all_to_all(blocks, axes, 0, 0, tiled=True)  5.78 us
    ppermute x10, waiting for transfers between devices, shifted(): lax.ppermute(block, axis, [(i, (i + by) % size) for i in range(size)])  5.64 us
    pallas_call x2, Pallas kernels, partial_images(): pl.pallas_call(images_kernel, grid_spec=pltpu.PrefetchScalarGridSpec(num_...  5.56 us
  transfers between devices with their start and end apart: 12, of which 6 were waited for; matrix products, arithmetic and copies ran while one was open for 1% of the time, Pallas kernels for 19%

profile of v2, /device:TPU:1, one launch (start us, length us, event | category | flops | bytes accessed | tf_op | source)
XLA Modules:
  0.0 163.4 jit_solution(7867721975242580841)
XLA Ops:
  0.7 1.9 %copy-done = f32[1536,512]{1,0:T(8,128)S(1)} copy-done((f32[1536,512]{1,0:T(8,128)S(1)}, f32[1536,512]{1,0:T(8,128)}, u32[]{:S(2)}) %copy-start) | copy-done | bytes 3145752
  2.6 1.2 copy-done.1
  3.8 2.8 %shard_map.42 = f32[768,512]{1,0:T(8,128)S(1)} custom-call(s32[2]{0:T(128)S(1)} %pad_add_fusion.place_ref, f32[1536,512]{1,0:T(8,128)S(1)} %copy-done, f32[512,512]{1,0:T(8,128)S(1)} %copy-done.1), custom_call_target="tpu_custom_call" | custom-call | flops 1207959552 | bytes 6291456 | tf_op jit(solution)/shard_map/pallas_call | solution.py:81
  6.6 8.8 %collective-permute-start = (f32[768,512]{1,0:T(8,128)S(1)}, f32[768,512]{1,0:T(8,128)S(1)}, u32[]{:S(2)}, u32[]{:S(2)}) collective-permute-start(f32[768,512]{1,0:T(8,128)S(1)} %shard_map.42), channel_id=1, source_target_pairs={{0,1},{1,0},{2,3},{3,2},{4,5},{5,4},{6,7},{7,6},{8,9},{9,8},{10,11... | collective-permute-start | bytes 4718600 | tf_op jit(solution)/shard_map/ppermute | solution.py:304
  15.4 2.8 %shard_map.41 = f32[768,512]{1,0:T(8,128)S(1)} custom-call(s32[2]{0:T(128)S(1)} %pad_add_fusion.place_ref, f32[1536,512]{1,0:T(8,128)S(1)} %copy-done, f32[512,512]{1,0:T(8,128)S(1)} %copy-done.1), custom_call_target="tpu_custom_call" | custom-call | flops 1207959552 | bytes 6291456 | tf_op jit(solution)/shard_map/pallas_call | solution.py:81
  18.2 0.2 collective-permute-done
  18.4 0.3 add.6
  18.8 22.9 %all_to_all.25 = f32[4,192,512]{2,1,0:T(8,128)S(1)} all-to-all(f32[4,192,512]{2,1,0:T(8,128)S(1)} %bitcast.16), channel_id=1, replica_groups=mesh['z'=8,'y'=8,'x'=4,'core'=2] {'x'}, dimensions={0} | all-to-all | bytes 3145728 | tf_op jit(solution)/shard_map/all_to_all | solution.py:294
  41.7 0.2 reduce_sum.36.images_ref.refs_8_
  41.9 1.2 shard_map.43
  43.0 3.1 %collective-permute-start.1 = (f32[256,512]{1,0:T(8,128)S(1)}, f32[256,512]{1,0:T(8,128)S(1)}, u32[]{:S(2)}, u32[]{:S(2)}) collective-permute-start(f32[256,512]{1,0:T(8,128)S(1)} %get-tuple-element.14), channel_id=1, source_target_pairs={{0,1},{1,0},{2,3},{3,2},{4,5},{5,4},{6,7},{7,6},{8,9},{9,8},{10,11... | collective-permute-start | bytes 1572872 | tf_op jit(solution)/shard_map/ppermute | solution.py:304
  46.1 1.5 collective-permute-done.1
  47.7 11.6 %all_to_all.26 = f32[4,64,512]{2,1,0:T(8,128)S(1)} all-to-all(f32[4,64,512]{2,1,0:T(8,128)S(1)} %bitcast.17), channel_id=1, replica_groups=mesh['z'=8,'y'=8,'x'=4,'core'=2] {'x'}, dimensions={0} | all-to-all | bytes 1048576 | tf_op jit(solution)/shard_map/all_to_all | solution.py:294
  59.5 2.2 %collective-permute-start.2 = (f32[192,512]{1,0:T(8,128)S(1)}, f32[192,512]{1,0:T(8,128)S(1)}, u32[]{:S(2)}, u32[]{:S(2)}) collective-permute-start(f32[192,512]{1,0:T(8,128)S(1)} %reduce_sum.36.images_ref.refs_8_), channel_id=1, source_target_pairs={{0,2},{2,4},{4,6},{6,0},{1,3},{3,5},{5,7},{7,1},{8,10},{10,12},{12... | collective-permute-start | bytes 1179656 | tf_op jit(solution)/shard_map/ppermute | solution.py:304
  61.7 3.7 %collective-permute-start.3 = (f32[192,512]{1,0:T(8,128)S(1)}, f32[192,512]{1,0:T(8,128)S(1)}, u32[]{:S(2)}, u32[]{:S(2)}) collective-permute-start(f32[192,512]{1,0:T(8,128)S(1)} %reduce_sum.36.images_ref.refs_8_), channel_id=1, source_target_pairs={{0,4},{2,6},{4,0},{6,2},{1,5},{3,7},{5,1},{7,3},{8,12},{10,14},{12... | collective-permute-start | bytes 1179656 | tf_op jit(solution)/shard_map/ppermute | solution.py:304
  65.4 2.5 %collective-permute-start.4 = (f32[192,512]{1,0:T(8,128)S(1)}, f32[192,512]{1,0:T(8,128)S(1)}, u32[]{:S(2)}, u32[]{:S(2)}) collective-permute-start(f32[192,512]{1,0:T(8,128)S(1)} %reduce_sum.36.images_ref.refs_8_), channel_id=1, source_target_pairs={{0,6},{2,0},{4,2},{6,4},{1,7},{3,1},{5,3},{7,5},{8,14},{10,8},{12,... | collective-permute-start | bytes 1179656 | tf_op jit(solution)/shard_map/ppermute | solution.py:304
  67.9 23.6 %all_to_all.27 = f32[64,4,128]{2,1,0:T(4,128)S(1)} all-to-all(f32[64,4,128]{2,1,0:T(4,128)S(1)} %reshape.22), channel_id=1, replica_groups=mesh['z'=8,'y'=8,'x'=4,'core'=2] {'z','y'}, dimensions={0} | all-to-all | bytes 262144 | tf_op jit(solution)/shard_map/all_to_all | solution.py:294
  91.6 1.3 pad_maximum_fusion
  92.9 5.4 %collective-permute-start.9 = (f32[768,512]{1,0:T(8,128)}, f32[768,512]{1,0:T(8,128)S(1)}, u32[]{:S(2)}, u32[]{:S(2)}) collective-permute-start(f32[768,512]{1,0:T(8,128)} %pad_maximum_fusion), channel_id=1, source_target_pairs={{0,1},{1,0},{2,3},{3,2},{4,5},{5,4},{6,7},{7,6},{8,9},{9,8},{10,11... | collective-permute-start | bytes 4718600 | tf_op jit(solution)/shard_map/ppermute | solution.py:304
  98.3 0.7 broadcast_in_dim.2
  98.9 4.6 %all-to-all-start.3 = ((f32[64,4,128]{2,1,0:T(4,128)}), f32[64,4,128]{2,1,0:T(4,128)S(1)}, u32[]{:S(2)}, u32[]{:S(2)}) async-start(f32[64,4,128]{2,1,0:T(4,128)} %broadcast_in_dim.2), calls=%async_computation.3 | async-start | bytes 262144 | tf_op jit(solution)/shard_map/all_to_all | solution.py:294
  103.7 6.0 %shard_map.45 = f32[512,512]{1,0:T(8,128)} custom-call(s32[2]{0:T(128)S(1)} %pad_add_fusion.place_ref, f32[1536,512]{1,0:T(8,128)} %refs_7_.1, f32[1536,512]{1,0:T(8,128)} %refs_7_.1, f32[1536,512]{1,0:T(8,128)} %refs_7_.1, f32[1536,512]{1,0:T(8,128)} %refs_7_.1, f32[1536,512]{1,0:T(8,128)} %refs_7_.1, f32[1536,512]{1,0:T(8,128)} %refs_7_.1, ...), custom_call_target="tpu_custom_call" | custom-call | flops 2415919104 | bytes 6291456 | tf_op jit(solution)/shard_map/pallas_call | solution.py:149
  109.7 5.8 %all-to-all-done.3 = f32[64,4,128]{2,1,0:T(4,128)S(1)} async-done(((f32[64,4,128]{2,1,0:T(4,128)}), f32[64,4,128]{2,1,0:T(4,128)S(1)}, u32[]{:S(2)}, u32[]{:S(2)}) %all-to-all-start.3) | async-done | bytes 131104 | tf_op jit(solution)/shard_map/all_to_all | solution.py:294
  115.5 6.4 %all-to-all-start.4 = ((f32[64,8,512]{2,1,0:T(8,128)}), f32[64,8,512]{2,1,0:T(8,128)S(1)}, u32[]{:S(2)}, u32[]{:S(2)}) async-start(f32[64,8,512]{2,1,0:T(8,128)} %bitcast.4), calls=%async_computation.4 | async-start | bytes 2097152 | tf_op jit(solution)/shard_map/all_to_all | solution.py:294
  121.9 2.8 %collective-permute-start.5 = (f32[64,512]{1,0:T(8,128)S(1)}, f32[64,512]{1,0:T(8,128)S(1)}, u32[]{:S(2)}, u32[]{:S(2)}) collective-permute-start(f32[64,512]{1,0:T(8,128)S(1)} %bitcast.11), channel_id=1, source_target_pairs={{0,2},{2,4},{4,6},{6,0},{1,3},{3,5},{5,7},{7,1},{8,10},{10,12},{12... | collective-permute-start | bytes 393224 | tf_op jit(solution)/shard_map/ppermute | solution.py:304
  124.7 3.4 %collective-permute-start.6 = (f32[64,512]{1,0:T(8,128)S(1)}, f32[64,512]{1,0:T(8,128)S(1)}, u32[]{:S(2)}, u32[]{:S(2)}) collective-permute-start(f32[64,512]{1,0:T(8,128)S(1)} %bitcast.12), channel_id=1, source_target_pairs={{0,4},{2,6},{4,0},{6,2},{1,5},{3,7},{5,1},{7,3},{8,12},{10,14},{12... | collective-permute-start | bytes 393224 | tf_op jit(solution)/shard_map/ppermute | solution.py:304
  128.2 4.0 %collective-permute-start.7 = (f32[64,512]{1,0:T(8,128)S(1)}, f32[64,512]{1,0:T(8,128)S(1)}, u32[]{:S(2)}, u32[]{:S(2)}) collective-permute-start(f32[64,512]{1,0:T(8,128)S(1)} %bitcast.13), channel_id=1, source_target_pairs={{0,6},{2,0},{4,2},{6,4},{1,7},{3,1},{5,3},{7,5},{8,14},{10,8},{12,... | collective-permute-start | bytes 393224 | tf_op jit(solution)/shard_map/ppermute | solution.py:304
  132.3 2.4 %collective-permute-done.7.refs_3_ = f32[64,512]{1,0:T(8,128)S(1)} collective-permute-done((f32[64,512]{1,0:T(8,128)S(1)}, f32[64,512]{1,0:T(8,128)S(1)}, u32[]{:S(2)}, u32[]{:S(2)}) %collective-permute-start.7) | collective-permute-done | bytes 131104 | tf_op jit(solution)/shard_map/ppermute | solution.py:304
  134.7 3.6 %collective-permute-start.8 = (f32[256,512]{1,0:T(8,128)S(1)}, f32[256,512]{1,0:T(8,128)S(1)}, u32[]{:S(2)}, u32[]{:S(2)}) collective-permute-start(f32[256,512]{1,0:T(8,128)S(1)} %pad_maximum_fusion.1), channel_id=1, source_target_pairs={{0,1},{1,0},{2,3},{3,2},{4,5},{5,4},{6,7},{7,6},{8,9},{9,8},{10,11... | collective-permute-start | bytes 1572872 | tf_op jit(solution)/shard_map/ppermute | solution.py:304
  138.4 1.3 collective-permute-done.8
  139.7 22.0 %shard_map.44 = (f32[512,512]{1,0:T(8,128)S(1)}, f32[192,512]{1,0:T(8,128)}) custom-call(s32[2]{0:T(128)S(1)} %pad_add_fusion.place_ref, f32[192,512]{1,0:T(8,128)S(1)} %reduce_sum.36.images_ref.refs_8_, f32[64,512]{1,0:T(8,128)S(1)} %bitcast.15, f32[64,512]{1,0:T(8,128)S(1)} %collective-permute-done.5.refs_1_, ...), custom_call_target="tpu_custom_call" | custom-call | flops 524288 | bytes 512 | tf_op jit(solution)/shard_map/pallas_call | solution.py:269
  161.8 1.6 fusion.2
  (19 shorter events, 0.8 us)
Async XLA Ops:
  0.7 1.9 %copy-start = (f32[1536,512]{1,0:T(8,128)S(1)}, f32[1536,512]{1,0:T(8,128)}, u32[]{:S(2)}) copy-start(f32[1536,512]{1,0:T(8,128)} %refs_7_.1) | copy-start | bytes 9437188
  2.6 1.2 copy-start.1
  6.6 11.8 %collective-permute-start = (f32[768,512]{1,0:T(8,128)S(1)}, f32[768,512]{1,0:T(8,128)S(1)}, u32[]{:S(2)}, u32[]{:S(2)}) collective-permute-start(f32[768,512]{1,0:T(8,128)S(1)} %shard_map.42), channel_id=1, source_target_pairs={{0,1},{1,0},{2,3},{3,2},{4,5},{5,4},{6,7},{7,6},{8,9},{9,8},{10,11... | collective-permute-start | bytes 4718600 | tf_op jit(solution)/shard_map/ppermute | solution.py:304
  43.0 4.6 %collective-permute-start.1 = (f32[256,512]{1,0:T(8,128)S(1)}, f32[256,512]{1,0:T(8,128)S(1)}, u32[]{:S(2)}, u32[]{:S(2)}) collective-permute-start(f32[256,512]{1,0:T(8,128)S(1)} %get-tuple-element.14), channel_id=1, source_target_pairs={{0,1},{1,0},{2,3},{3,2},{4,5},{5,4},{6,7},{7,6},{8,9},{9,8},{10,11... | collective-permute-start | bytes 1572872 | tf_op jit(solution)/shard_map/ppermute | solution.py:304
  59.5 32.2 %collective-permute-start.2 = (f32[192,512]{1,0:T(8,128)S(1)}, f32[192,512]{1,0:T(8,128)S(1)}, u32[]{:S(2)}, u32[]{:S(2)}) collective-permute-start(f32[192,512]{1,0:T(8,128)S(1)} %reduce_sum.36.images_ref.refs_8_), channel_id=1, source_target_pairs={{0,2},{2,4},{4,6},{6,0},{1,3},{3,5},{5,7},{7,1},{8,10},{10,12},{12... | collective-permute-start | bytes 1179656 | tf_op jit(solution)/shard_map/ppermute | solution.py:304
  61.7 30.0 %collective-permute-start.3 = (f32[192,512]{1,0:T(8,128)S(1)}, f32[192,512]{1,0:T(8,128)S(1)}, u32[]{:S(2)}, u32[]{:S(2)}) collective-permute-start(f32[192,512]{1,0:T(8,128)S(1)} %reduce_sum.36.images_ref.refs_8_), channel_id=1, source_target_pairs={{0,4},{2,6},{4,0},{6,2},{1,5},{3,7},{5,1},{7,3},{8,12},{10,14},{12... | collective-permute-start | bytes 1179656 | tf_op jit(solution)/shard_map/ppermute | solution.py:304
  65.4 26.3 %collective-permute-start.4 = (f32[192,512]{1,0:T(8,128)S(1)}, f32[192,512]{1,0:T(8,128)S(1)}, u32[]{:S(2)}, u32[]{:S(2)}) collective-permute-start(f32[192,512]{1,0:T(8,128)S(1)} %reduce_sum.36.images_ref.refs_8_), channel_id=1, source_target_pairs={{0,6},{2,0},{4,2},{6,4},{1,7},{3,1},{5,3},{7,5},{8,14},{10,8},{12,... | collective-permute-start | bytes 1179656 | tf_op jit(solution)/shard_map/ppermute | solution.py:304
  92.9 10.7 %collective-permute-start.9 = (f32[768,512]{1,0:T(8,128)}, f32[768,512]{1,0:T(8,128)S(1)}, u32[]{:S(2)}, u32[]{:S(2)}) collective-permute-start(f32[768,512]{1,0:T(8,128)} %pad_maximum_fusion), channel_id=1, source_target_pairs={{0,1},{1,0},{2,3},{3,2},{4,5},{5,4},{6,7},{7,6},{8,9},{9,8},{10,11... | collective-permute-start | bytes 4718600 | tf_op jit(solution)/shard_map/ppermute | solution.py:304
  98.9 16.6 %all-to-all-start.3 = ((f32[64,4,128]{2,1,0:T(4,128)}), f32[64,4,128]{2,1,0:T(4,128)S(1)}, u32[]{:S(2)}, u32[]{:S(2)}) async-start(f32[64,4,128]{2,1,0:T(4,128)} %broadcast_in_dim.2), calls=%async_computation.3 | async-start | bytes 262144 | tf_op jit(solution)/shard_map/all_to_all | solution.py:294
  115.5 46.2 %all-to-all-start.4 = ((f32[64,8,512]{2,1,0:T(8,128)}), f32[64,8,512]{2,1,0:T(8,128)S(1)}, u32[]{:S(2)}, u32[]{:S(2)}) async-start(f32[64,8,512]{2,1,0:T(8,128)} %bitcast.4), calls=%async_computation.4 | async-start | bytes 2097152 | tf_op jit(solution)/shard_map/all_to_all | solution.py:294
  121.9 10.3 %collective-permute-start.5 = (f32[64,512]{1,0:T(8,128)S(1)}, f32[64,512]{1,0:T(8,128)S(1)}, u32[]{:S(2)}, u32[]{:S(2)}) collective-permute-start(f32[64,512]{1,0:T(8,128)S(1)} %bitcast.11), channel_id=1, source_target_pairs={{0,2},{2,4},{4,6},{6,0},{1,3},{3,5},{5,7},{7,1},{8,10},{10,12},{12... | collective-permute-start | bytes 393224 | tf_op jit(solution)/shard_map/ppermute | solution.py:304
  124.7 7.6 %collective-permute-start.6 = (f32[64,512]{1,0:T(8,128)S(1)}, f32[64,512]{1,0:T(8,128)S(1)}, u32[]{:S(2)}, u32[]{:S(2)}) collective-permute-start(f32[64,512]{1,0:T(8,128)S(1)} %bitcast.12), channel_id=1, source_target_pairs={{0,4},{2,6},{4,0},{6,2},{1,5},{3,7},{5,1},{7,3},{8,12},{10,14},{12... | collective-permute-start | bytes 393224 | tf_op jit(solution)/shard_map/ppermute | solution.py:304
  128.2 6.5 %collective-permute-start.7 = (f32[64,512]{1,0:T(8,128)S(1)}, f32[64,512]{1,0:T(8,128)S(1)}, u32[]{:S(2)}, u32[]{:S(2)}) collective-permute-start(f32[64,512]{1,0:T(8,128)S(1)} %bitcast.13), channel_id=1, source_target_pairs={{0,6},{2,0},{4,2},{6,4},{1,7},{3,1},{5,3},{7,5},{8,14},{10,8},{12,... | collective-permute-start | bytes 393224 | tf_op jit(solution)/shard_map/ppermute | solution.py:304
  134.7 4.9 %collective-permute-start.8 = (f32[256,512]{1,0:T(8,128)S(1)}, f32[256,512]{1,0:T(8,128)S(1)}, u32[]{:S(2)}, u32[]{:S(2)}) collective-permute-start(f32[256,512]{1,0:T(8,128)S(1)} %pad_maximum_fusion.1), channel_id=1, source_target_pairs={{0,1},{1,0},{2,3},{3,2},{4,5},{5,4},{6,7},{7,6},{8,9},{9,8},{10,11... | collective-permute-start | bytes 1572872 | tf_op jit(solution)/shard_map/ppermute | solution.py:304

commit v3 on v2

--- a/solution.py
+++ b/solution.py
@@ -11,7 +11,8 @@
 
 CORES = 2
 BLOCK = 128
-GROUP = 4
+GROUP = 2
+AHEAD = 2
 F32 = jnp.float32
 BF16 = jnp.bfloat16
 HIGHEST = lax.Precision.HIGHEST
@@ -102,17 +103,36 @@
     return pl.BlockSpec(shape, lambda i, place: (0,) * len(shape))
 
 
+def upper_blocks(size):
+    count = size // BLOCK
+    return [(i, j) for i in range(count) for j in range(i, count)]
+
+
 def gram_kernel(place_ref, images_ref, kept_ref, sent_ref):
-    rows = kept_ref.shape[0]
-    images = halves(images_ref[...])
-    for core, out_ref in ((place_ref[0], kept_ref), (1 - place_ref[0], sent_ref)):
-        columns = pl.ds(pl.multiple_of(core * rows, rows), rows)
-        out_ref[...] = three_pass_dot([halves(images_ref[:, columns])], [images], 0, 0)
+    high, low = halves(images_ref[...])
+    left = jnp.concatenate([high, low, high], 0)
+    right = jnp.concatenate([high, high, low], 0)
+    size = left.shape[1]
+    blocks = []
+    for first in range(0, size, BLOCK):
+        panel = lax.dot_general(
+            left[:, first : first + BLOCK],
+            right[:, first:],
+            (((0,), (0,)), ((), ())),
+            preferred_element_type=F32,
+        )
+        blocks += [panel[:, at : at + BLOCK] for at in range(0, size - first, BLOCK)]
+    per = len(blocks) // CORES
+    is_first = place_ref[0] == 0
+    for n in range(per):
+        rows = pl.ds(n * BLOCK, BLOCK)
+        kept_ref[rows, :] = jnp.where(is_first, blocks[n], blocks[per + n])
+        sent_ref[rows, :] = jnp.where(is_first, blocks[per + n], blocks[n])
 
 
 def gram_halves(images, place):
     rows, width = images.shape
-    shape = (width // CORES, width)
+    shape = (len(upper_blocks(width)) // CORES * BLOCK, BLOCK)
     return pl.pallas_call(
         gram_kernel,
         grid_spec=pltpu.PrefetchScalarGridSpec(
@@ -178,89 +198,91 @@
 
     for group in range(0, count, GROUP):
         end = group + GROUP
+        reach = min(end + AHEAD, count)
         finished = []
         for p in range(group, end):
-            panel = rows[p]
-            columns = [column(panel, 8 * p + j) for j in range(8)]
+            panel, base = rows[p], 8 * p
+            own = (lane >= base) & (lane < base + 8)
+            columns = [column(panel, base + j) for j in range(8)]
+            small = [[row(columns[k], i) for k in range(i + 1)] for i in range(8)]
+            across = [
+                jnp.where(lane == base + j, 1.0, jnp.where(own, 0.0, row(panel, j))) for j in range(8)
+            ]
+            later = range(p + 1, reach)
+            down = {i: [column(rows[i], base + j) for j in range(8)] for i in later}
+            for i in later:
+                rows[i] = jnp.where(own, 0.0, rows[i])
             kept = jnp.zeros(shape, F32)
             pivots = jnp.zeros(shape, F32)
             for j in range(8):
-                here = lane == 8 * p + j
-                at = sub == j
-                pivot = row(columns[j], j)
-                inverse = 1.0 / pivot
-                current = jnp.where(here, 1.0, row(panel, j))
-                kept = jnp.where(at, current, kept)
-                pivots = jnp.where(at, pivot, pivots)
-                scaled = current * inverse
-                panel = jnp.where(at, scaled, jnp.where(here, 0.0, panel) - columns[j] * scaled)
-                for k in range(j + 1, 8):
-                    part = row(columns[k], j) * inverse
-                    columns[k] = jnp.where(at, part, columns[k] - columns[j] * part)
+                inverse = 1.0 / small[j][j]
+                ratio = {i: small[i][j] * inverse for i in range(j + 1, 8)}
+                for i in range(j + 1, 8):
+                    for k in range(j + 1, i + 1):
+                        small[i][k] = small[i][k] - ratio[i] * small[k][j]
+                    across[i] = across[i] - ratio[i] * across[j]
+                scaled = across[j] * inverse
+                for i in later:
+                    for k in range(j + 1, 8):
+                        down[i][k] = down[i][k] - down[i][j] * ratio[k]
+                    rows[i] = rows[i] - down[i][j] * scaled
+                kept = jnp.where(sub == j, across[j], kept)
+                pivots = jnp.where(sub == j, small[j][j], pivots)
             finished.append(kept * lax.rsqrt(pivots))
-            own = (lane >= 8 * p) & (lane < 8 * p + 8)
-            spread = [row(panel, j) for j in range(8)]
-            for i in range(p + 1, end):
-                terms = [column(rows[i], 8 * p + j) * spread[j] for j in range(8)]
-                while len(terms) > 1:
-                    terms = [terms[a] + terms[a + 1] for a in range(0, len(terms), 2)]
-                rows[i] = jnp.where(own, 0.0, rows[i]) - terms[0]
         lower = [lane <= sub + 8 * p for p in range(group, end)]
         result += [jnp.where(keep, slab, 0.0) for keep, slab in zip(lower, finished)]
-        if end < count:
-            later = lane >= 8 * end
+        if reach < count:
+            right = lane >= 8 * end
             panel = jnp.concatenate(
-                [jnp.where(keep | later, slab, 0.0) for keep, slab in zip(lower, finished)], 0
+                [jnp.where(keep | right, slab, 0.0) for keep, slab in zip(lower, finished)], 0
             )
             change = six_pass_dot(panel, panel, 0, 0)
             own = (lane >= 8 * group) & (lane < 8 * end)
-            for i in range(end, count):
+            for i in range(reach, count):
                 rows[i] = jnp.where(own, 0.0, rows[i]) - change[8 * i : 8 * i + 8]
     return result
 
 
 def factor_kernel(scale, groups, place_ref, images_ref, *refs):
     gram_refs = refs[: 2 * groups]
-    inverse_ref, basis_ref, work_ref, small_ref, panel_ref = refs[2 * groups :]
+    inverse_ref, basis_ref, packed_ref, work_ref = refs[2 * groups :]
     size = work_ref.shape[0]
-    blocks = size // BLOCK
     slab = gram_refs[0].shape[0]
     for flip in range(CORES):
         core = 1 - place_ref[0] if flip else place_ref[0]
         for shift in range(groups):
             owner = lax.rem(place_ref[1] - shift + groups, groups)
             first = pl.multiple_of((core * groups + owner) * slab, slab)
-            work_ref[pl.ds(first, slab), :] = gram_refs[flip * groups + shift][...]
-    column = lax.broadcasted_iota(jnp.int32, (BLOCK, size), 1)
+            packed_ref[pl.ds(first, slab), :] = gram_refs[flip * groups + shift][...]
+    work_ref[...] = jnp.zeros_like(work_ref)
+    for n, (i, j) in enumerate(upper_blocks(size)):
+        work_ref[i * BLOCK : (i + 1) * BLOCK, j * BLOCK : (j + 1) * BLOCK] = packed_ref[
+            n * BLOCK : (n + 1) * BLOCK, :
+        ]
     unit = (
         lax.broadcasted_iota(jnp.int32, (BLOCK, BLOCK), 0)
         == lax.broadcasted_iota(jnp.int32, (BLOCK, BLOCK), 1)
     ).astype(F32)
 
-    def block_step(k, carry):
-        first = pl.multiple_of(k * BLOCK, BLOCK)
-        here = pl.ds(first, BLOCK)
-        slabs = factor_block([work_ref[pl.ds(first + 8 * i, 8), here] for i in range(BLOCK // 8)])
-        for i, rows in enumerate(slabs):
-            small_ref[8 * i : 8 * i + 8, :] = rows
-        work_ref[here, here] = unit
-        panel = six_pass_dot(small_ref[...], work_ref[here, :], 1, 0)
-        panel_ref[...] = panel
-        finished = jnp.where(column < first + BLOCK, panel, 0.0)
-        inverse_ref[here, :] = finished
-        own = (column >= first) & (column < first + BLOCK)
-
-        def update(i, inner):
-            there = pl.ds(pl.multiple_of(i * BLOCK, BLOCK), BLOCK)
-            kept = jnp.where(own, 0.0, work_ref[there, :])
-            work_ref[there, :] = kept - six_pass_dot(panel_ref[:, there], panel_ref[...], 0, 0)
-            return inner
-
-        lax.fori_loop(k + 1, blocks, update, 0)
-        basis_ref[:, here] = scale * six_pass_dot(images_ref[...], finished, 1, 1)
-        return carry
-
-    lax.fori_loop(0, blocks, block_step, 0)
+    diagonal = packed_ref[:BLOCK, :]
+    for first in range(0, size, BLOCK):
+        end = first + BLOCK
+        slabs = factor_block([diagonal[8 * i : 8 * i + 8] for i in range(BLOCK // 8)])
+        work_ref[first:end, first:end] = unit
+        panel = six_pass_dot(jnp.concatenate(slabs, 0), work_ref[first:end, :], 1, 0)
+        finished = panel[:, :end]
+        if end < size:
+            following = panel[:, end : end + BLOCK]
+            diagonal = work_ref[end : end + BLOCK, end : end + BLOCK]
+            diagonal = diagonal - six_pass_dot(following, following, 0, 0)
+            change = six_pass_dot(panel[:, end:], panel, 0, 0)
+            if first:
+                work_ref[end:, :first] = work_ref[end:, :first] - change[:, :first]
+            work_ref[end:, first:end] = -change[:, first:end]
+            work_ref[end:, end:] = work_ref[end:, end:] - change[:, end:]
+            inverse_ref[first:end, end:] = jnp.zeros((BLOCK, size - end), F32)
+        inverse_ref[first:end, :end] = finished
+        basis_ref[:, first:end] = scale * six_pass_dot(images_ref[:, :end], finished, 1, 1)
 
 
 def factor(pieces, images, place, scale):
@@ -274,9 +296,8 @@
             in_specs=[whole(part.shape) for part in (images, *pieces)],
             out_specs=[whole((size, size)), whole(images.shape)],
             scratch_shapes=[
+                pltpu.VMEM((len(upper_blocks(size)) * BLOCK, BLOCK), F32),
                 pltpu.VMEM((size, size), F32),
-                pltpu.VMEM((BLOCK, BLOCK), F32),
-                pltpu.VMEM((BLOCK, size), F32),
             ],
         ),
         out_shape=[
@@ -311,7 +332,7 @@
     rows_here = archive.shape[0]
     width = sketch.shape[1]
     own_rows = rows_here // (groups * CORES)
-    slab_rows = width // (groups * CORES)
+    slab_rows = len(upper_blocks(width)) * BLOCK // (groups * CORES)
     scale = math.sqrt(rows_here * stacked)
     place = jnp.stack([lax.axis_index("core"), lax.axis_index("x")]).astype(jnp.int32)
 
@@ -322,18 +343,18 @@
 
     kept, sent = gram_halves(own, place)
     gram = kept + shifted(sent, "core", 1)
-    gram = exchange(gram.reshape(groups, slab_rows, width), "x").sum(0)
-    split = gram.reshape(stacked, -1, BLOCK)
-    split, late = lax.optimization_barrier((split, own))
-    row = exchange(split, over_rows).sum(0).reshape(split.shape[1:])
-
-    near = [late, *(shifted(late, "x", s) for s in range(1, groups))]
+    gram = exchange(gram.reshape(groups, slab_rows, BLOCK), "x").sum(0)
+    per = pl.cdiv(slab_rows, stacked)
+    split = jnp.pad(gram, ((0, per * stacked - slab_rows), (0, 0))).reshape(stacked, per, BLOCK)
+    row = exchange(split, over_rows).sum(0)
+
+    near = [own, *(shifted(own, "x", s) for s in range(1, groups))]
     row, near = lax.optimization_barrier((row, near))
     far = shifted(jnp.concatenate(near, 0), "core", 1)
     far = [far[s * own_rows : (s + 1) * own_rows] for s in range(groups)]
     moved = moved_rows(archive, near, far, place, groups)
 
-    gram = gather(row, over_rows).reshape(slab_rows, width)
+    gram = gather(row, over_rows).reshape(per * stacked, BLOCK)[:slab_rows]
     moved = exchange(moved.reshape(stacked, -1, width), over_rows)
     here = [gram, *(shifted(gram, "x", s) for s in range(1, groups))]
     there = shifted(jnp.concatenate(here, 0), "core", 1)

time: 164 us -> 153 us (0.933)
  blocking collectives: 58.2 us -> 46.6 us
  Pallas kernels: 34.7 us -> 31 us
  starting transfers between devices: 50.5 us -> 53.9 us
    all_to_all x3 -> x2, blocking collectives: 58.2 us -> 46.6 us  [exchange(): return lax.all_to_all(blocks, axes, 0, 0, tiled=True)]
    pallas_call x1, Pallas kernels: 22 us -> 18.4 us  [factor(): pl.pallas_call(functools.partial(factor_kernel, scale, len(pieces) // COR...]
    all_to_all x2 -> x3, starting transfers between devices: 11 us -> 14.4 us  [exchange(): return lax.all_to_all(blocks, axes, 0, 0, tiled=True)]
    all_to_all x2 -> x3, waiting for transfers between devices: 5.78 us -> 5.77 us  [exchange(): return lax.all_to_all(blocks, axes, 0, 0, tiled=True)]
  transfers between devices with their start and end apart: 12 -> 13, of which waited for: 6 -> 6; matrix products, arithmetic and copies ran while one was open for 1% -> 1% of each run, Pallas kernels for 19% -> 18%
where the time goes in v3:
time: 153 us; the launch traced here: 152 us
  starting transfers between devices  53.9 us (35%)
  blocking collectives  46.6 us (30%)
  Pallas kernels  31 us (20%)
  waiting for transfers between devices  11.2 us (7%)
  local copies, waits for them, and re-layouts  4.04 us (3%)
  other arithmetic  2.85 us (2%)
  matrix products  1.58 us (1%)
    all_to_all x2, blocking collectives, exchange(): return lax.all_to_all(blocks, axes, 0, 0, tiled=True)  46.6 us
    ppermute x10, starting transfers between devices, shifted(): lax.ppermute(block, axis, [(i, (i + by) % size) for i in range(size)])  39.4 us
    pallas_call x1, Pallas kernels, factor(): pl.pallas_call(functools.partial(factor_kernel, scale, len(pieces) // COR...  18.4 us
    all_to_all x3, starting transfers between devices, exchange(): return lax.all_to_all(blocks, axes, 0, 0, tiled=True)  14.4 us
    pallas_call x1, Pallas kernels, moved_rows(): pl.pallas_call(functools.partial(moved_kernel, len(images)), grid_spec=pl...  6.03 us
    all_to_all x3, waiting for transfers between devices, exchange(): return lax.all_to_all(blocks, axes, 0, 0, tiled=True)  5.77 us
    pallas_call x2, Pallas kernels, partial_images(): pl.pallas_call(images_kernel, grid_spec=pltpu.PrefetchScalarGridSpec(num_...  5.56 us
    ppermute x10, waiting for transfers between devices, shifted(): lax.ppermute(block, axis, [(i, (i + by) % size) for i in range(size)])  5.45 us
  transfers between devices with their start and end apart: 13, of which 6 were waited for; matrix products, arithmetic and copies ran while one was open for 1% of the time, Pallas kernels for 18%

profile of v3, /device:TPU:1, one launch (start us, length us, event | category | flops | bytes accessed | tf_op | source)
XLA Modules:
  0.0 152.0 jit_solution(8454624321295088759)
XLA Ops:
  0.7 1.9 %copy-done = f32[1536,512]{1,0:T(8,128)S(1)} copy-done((f32[1536,512]{1,0:T(8,128)S(1)}, f32[1536,512]{1,0:T(8,128)}, u32[]{:S(2)}) %copy-start) | copy-done | bytes 3145752
  2.6 1.2 copy-done.1
  3.8 2.8 %shard_map.42 = f32[768,512]{1,0:T(8,128)S(1)} custom-call(s32[2]{0:T(128)S(1)} %pad_add_fusion.place_ref, f32[1536,512]{1,0:T(8,128)S(1)} %copy-done, f32[512,512]{1,0:T(8,128)S(1)} %copy-done.1), custom_call_target="tpu_custom_call" | custom-call | flops 1207959552 | bytes 6291456 | tf_op jit(solution)/shard_map/pallas_call | solution.py:82
  6.6 8.8 %collective-permute-start = (f32[768,512]{1,0:T(8,128)S(1)}, f32[768,512]{1,0:T(8,128)S(1)}, u32[]{:S(2)}, u32[]{:S(2)}) collective-permute-start(f32[768,512]{1,0:T(8,128)S(1)} %shard_map.42), channel_id=1, source_target_pairs={{0,1},{1,0},{2,3},{3,2},{4,5},{5,4},{6,7},{7,6},{8,9},{9,8},{10,11... | collective-permute-start | bytes 4718600 | tf_op jit(solution)/shard_map/ppermute | solution.py:325
  15.4 2.8 %shard_map.41 = f32[768,512]{1,0:T(8,128)S(1)} custom-call(s32[2]{0:T(128)S(1)} %pad_add_fusion.place_ref, f32[1536,512]{1,0:T(8,128)S(1)} %copy-done, f32[512,512]{1,0:T(8,128)S(1)} %copy-done.1), custom_call_target="tpu_custom_call" | custom-call | flops 1207959552 | bytes 6291456 | tf_op jit(solution)/shard_map/pallas_call | solution.py:82
  18.4 0.3 add.8
  18.8 22.9 %all_to_all.25 = f32[4,192,512]{2,1,0:T(8,128)S(1)} all-to-all(f32[4,192,512]{2,1,0:T(8,128)S(1)} %bitcast.7), channel_id=1, replica_groups=mesh['z'=8,'y'=8,'x'=4,'core'=2] {'x'}, dimensions={0} | all-to-all | bytes 3145728 | tf_op jit(solution)/shard_map/all_to_all | solution.py:315
  41.9 1.0 shard_map.43
  42.9 3.1 %collective-permute-start.1 = (f32[640,128]{1,0:T(8,128)S(1)}, f32[640,128]{1,0:T(8,128)S(1)}, u32[]{:S(2)}, u32[]{:S(2)}) collective-permute-start(f32[640,128]{1,0:T(8,128)S(1)} %get-tuple-element.12), channel_id=1, source_target_pairs={{0,1},{1,0},{2,3},{3,2},{4,5},{5,4},{6,7},{7,6},{8,9},{9,8},{10,11... | collective-permute-start | bytes 983048 | tf_op jit(solution)/shard_map/ppermute | solution.py:325
  46.0 1.2 collective-permute-done.1
  47.2 0.8 add.9
  48.0 3.5 %all-to-all-start.1 = ((f32[4,160,128]{2,1,0:T(8,128)}), f32[4,160,128]{2,1,0:T(8,128)S(1)}, u32[]{:S(2)}, u32[]{:S(2)}) async-start(f32[4,160,128]{2,1,0:T(8,128)} %bitcast.3), calls=%async_computation.1 | async-start | bytes 655360 | tf_op jit(solution)/shard_map/all_to_all | solution.py:315
  51.5 3.3 %collective-permute-start.2 = (f32[192,512]{1,0:T(8,128)S(1)}, f32[192,512]{1,0:T(8,128)S(1)}, u32[]{:S(2)}, u32[]{:S(2)}) collective-permute-start(f32[192,512]{1,0:T(8,128)S(1)} %reduce_sum.36.images_ref.refs_8_), channel_id=1, source_target_pairs={{0,2},{2,4},{4,6},{6,0},{1,3},{3,5},{5,7},{7,1},{8,10},{10,12},{12... | collective-permute-start | bytes 1179656 | tf_op jit(solution)/shard_map/ppermute | solution.py:325
  54.8 4.3 %collective-permute-start.3 = (f32[192,512]{1,0:T(8,128)S(1)}, f32[192,512]{1,0:T(8,128)S(1)}, u32[]{:S(2)}, u32[]{:S(2)}) collective-permute-start(f32[192,512]{1,0:T(8,128)S(1)} %reduce_sum.36.images_ref.refs_8_), channel_id=1, source_target_pairs={{0,4},{2,6},{4,0},{6,2},{1,5},{3,7},{5,1},{7,3},{8,12},{10,14},{12... | collective-permute-start | bytes 1179656 | tf_op jit(solution)/shard_map/ppermute | solution.py:325
  59.1 3.1 %collective-permute-start.4 = (f32[192,512]{1,0:T(8,128)S(1)}, f32[192,512]{1,0:T(8,128)S(1)}, u32[]{:S(2)}, u32[]{:S(2)}) collective-permute-start(f32[192,512]{1,0:T(8,128)S(1)} %reduce_sum.36.images_ref.refs_8_), channel_id=1, source_target_pairs={{0,6},{2,0},{4,2},{6,4},{1,7},{3,1},{5,3},{7,5},{8,14},{10,8},{12,... | collective-permute-start | bytes 1179656 | tf_op jit(solution)/shard_map/ppermute | solution.py:325
  62.3 23.7 %all_to_all.26 = f32[64,3,128]{2,1,0:T(4,128)S(1)} all-to-all(f32[64,3,128]{2,1,0:T(4,128)S(1)} %reshape.22), channel_id=1, replica_groups=mesh['z'=8,'y'=8,'x'=4,'core'=2] {'z','y'}, dimensions={0} | all-to-all | bytes 196608 | tf_op jit(solution)/shard_map/all_to_all | solution.py:315
  86.1 1.3 pad_maximum_fusion
  87.3 4.9 %collective-permute-start.9 = (f32[768,512]{1,0:T(8,128)}, f32[768,512]{1,0:T(8,128)S(1)}, u32[]{:S(2)}, u32[]{:S(2)}) collective-permute-start(f32[768,512]{1,0:T(8,128)} %pad_maximum_fusion), channel_id=1, source_target_pairs={{0,1},{1,0},{2,3},{3,2},{4,5},{5,4},{6,7},{7,6},{8,9},{9,8},{10,11... | collective-permute-start | bytes 4718600 | tf_op jit(solution)/shard_map/ppermute | solution.py:325
  92.2 0.7 broadcast_in_dim.2
  92.9 4.6 %all-to-all-start.3 = ((f32[64,3,128]{2,1,0:T(4,128)}), f32[64,3,128]{2,1,0:T(4,128)S(1)}, u32[]{:S(2)}, u32[]{:S(2)}) async-start(f32[64,3,128]{2,1,0:T(4,128)} %broadcast_in_dim.2), calls=%async_computation.3 | async-start | bytes 262144 | tf_op jit(solution)/shard_map/all_to_all | solution.py:315
  97.6 6.0 %shard_map.45 = f32[512,512]{1,0:T(8,128)} custom-call(s32[2]{0:T(128)S(1)} %pad_add_fusion.place_ref, f32[1536,512]{1,0:T(8,128)} %refs_7_.1, f32[1536,512]{1,0:T(8,128)} %refs_7_.1, f32[1536,512]{1,0:T(8,128)} %refs_7_.1, f32[1536,512]{1,0:T(8,128)} %refs_7_.1, f32[1536,512]{1,0:T(8,128)} %refs_7_.1, f32[1536,512]{1,0:T(8,128)} %refs_7_.1, ...), custom_call_target="tpu_custom_call" | custom-call | flops 2415919104 | bytes 6291456 | tf_op jit(solution)/shard_map/pallas_call | solution.py:169
  103.7 5.8 %all-to-all-done.3 = f32[64,3,128]{2,1,0:T(4,128)S(1)} async-done(((f32[64,3,128]{2,1,0:T(4,128)}), f32[64,3,128]{2,1,0:T(4,128)S(1)}, u32[]{:S(2)}, u32[]{:S(2)}) %all-to-all-start.3) | async-done | bytes 98336 | tf_op jit(solution)/shard_map/all_to_all | solution.py:315
  109.4 6.4 %all-to-all-start.4 = ((f32[64,8,512]{2,1,0:T(8,128)}), f32[64,8,512]{2,1,0:T(8,128)S(1)}, u32[]{:S(2)}, u32[]{:S(2)}) async-start(f32[64,8,512]{2,1,0:T(8,128)} %bitcast.4), calls=%async_computation.4 | async-start | bytes 2097152 | tf_op jit(solution)/shard_map/all_to_all | solution.py:315
  115.9 2.2 %collective-permute-start.5 = (f32[160,128]{1,0:T(8,128)S(1)}, f32[160,128]{1,0:T(8,128)S(1)}, u32[]{:S(2)}, u32[]{:S(2)}) collective-permute-start(f32[160,128]{1,0:T(8,128)S(1)} %slice.36.refs_0_), channel_id=1, source_target_pairs={{0,2},{2,4},{4,6},{6,0},{1,3},{3,5},{5,7},{7,1},{8,10},{10,12},{12... | collective-permute-start | bytes 245768 | tf_op jit(solution)/shard_map/ppermute | solution.py:325
  118.1 2.5 %collective-permute-start.6 = (f32[160,128]{1,0:T(8,128)S(1)}, f32[160,128]{1,0:T(8,128)S(1)}, u32[]{:S(2)}, u32[]{:S(2)}) collective-permute-start(f32[160,128]{1,0:T(8,128)S(1)} %slice.36.refs_0_), channel_id=1, source_target_pairs={{0,4},{2,6},{4,0},{6,2},{1,5},{3,7},{5,1},{7,3},{8,12},{10,14},{12... | collective-permute-start | bytes 245768 | tf_op jit(solution)/shard_map/ppermute | solution.py:325
  120.7 3.7 %collective-permute-start.7 = (f32[160,128]{1,0:T(8,128)S(1)}, f32[160,128]{1,0:T(8,128)S(1)}, u32[]{:S(2)}, u32[]{:S(2)}) collective-permute-start(f32[160,128]{1,0:T(8,128)S(1)} %slice.36.refs_0_), channel_id=1, source_target_pairs={{0,6},{2,0},{4,2},{6,4},{1,7},{3,1},{5,3},{7,5},{8,14},{10,8},{12,... | collective-permute-start | bytes 245768 | tf_op jit(solution)/shard_map/ppermute | solution.py:325
  124.3 0.7 collective-permute-done.6.refs_2_
  125.1 2.2 %collective-permute-done.7.refs_3_ = f32[160,128]{1,0:T(8,128)S(1)} collective-permute-done((f32[160,128]{1,0:T(8,128)S(1)}, f32[160,128]{1,0:T(8,128)S(1)}, u32[]{:S(2)}, u32[]{:S(2)}) %collective-permute-start.7) | collective-permute-done | bytes 81952 | tf_op jit(solution)/shard_map/ppermute | solution.py:325
  127.3 3.5 %collective-permute-start.8 = (f32[640,128]{1,0:T(8,128)S(1)}, f32[640,128]{1,0:T(8,128)S(1)}, u32[]{:S(2)}, u32[]{:S(2)}) collective-permute-start(f32[640,128]{1,0:T(8,128)S(1)} %pad_maximum_fusion.1), channel_id=1, source_target_pairs={{0,1},{1,0},{2,3},{3,2},{4,5},{5,4},{6,7},{7,6},{8,9},{9,8},{10,11... | collective-permute-start | bytes 983048 | tf_op jit(solution)/shard_map/ppermute | solution.py:325
  130.8 1.1 collective-permute-done.8
  131.9 18.4 %shard_map.44 = (f32[512,512]{1,0:T(8,128)S(1)}, f32[192,512]{1,0:T(8,128)}) custom-call(s32[2]{0:T(128)S(1)} %pad_add_fusion.place_ref, f32[192,512]{1,0:T(8,128)S(1)} %reduce_sum.36.images_ref.refs_8_, f32[160,128]{1,0:T(8,128)S(1)} %slice.36.refs_0_, f32[160,128]{1,0:T(8,128)S(1)} %collective-permute-done.5.refs_1_, ...), custom_call_target="tpu_custom_call" | custom-call | flops 524288 | bytes 512 | tf_op jit(solution)/shard_map/pallas_call | solution.py:291
  150.4 1.6 %fusion.2 = f32[8,512]{1,0:T(8,128)} fusion(f32[8,512]{1,0:T(8,128)S(1)} %reduce_sum.39, f32[512,512]{1,0:T(8,128)S(1)} %get-tuple-element.19), kind=kOutput, calls=%fused_computation.5 | convolution fusion | flops 25165824 | bytes 1081344 | tf_op jit(solution)/shard_map/dot_general | solution.py:23
  (22 shorter events, 1.0 us)
Async XLA Ops:
  0.7 1.9 %copy-start = (f32[1536,512]{1,0:T(8,128)S(1)}, f32[1536,512]{1,0:T(8,128)}, u32[]{:S(2)}) copy-start(f32[1536,512]{1,0:T(8,128)} %refs_7_.1) | copy-start | bytes 9437188
  2.6 1.2 copy-start.1
  6.6 11.8 %collective-permute-start = (f32[768,512]{1,0:T(8,128)S(1)}, f32[768,512]{1,0:T(8,128)S(1)}, u32[]{:S(2)}, u32[]{:S(2)}) collective-permute-start(f32[768,512]{1,0:T(8,128)S(1)} %shard_map.42), channel_id=1, source_target_pairs={{0,1},{1,0},{2,3},{3,2},{4,5},{5,4},{6,7},{7,6},{8,9},{9,8},{10,11... | collective-permute-start | bytes 4718600 | tf_op jit(solution)/shard_map/ppermute | solution.py:325
  42.9 4.4 %collective-permute-start.1 = (f32[640,128]{1,0:T(8,128)S(1)}, f32[640,128]{1,0:T(8,128)S(1)}, u32[]{:S(2)}, u32[]{:S(2)}) collective-permute-start(f32[640,128]{1,0:T(8,128)S(1)} %get-tuple-element.12), channel_id=1, source_target_pairs={{0,1},{1,0},{2,3},{3,2},{4,5},{5,4},{6,7},{7,6},{8,9},{9,8},{10,11... | collective-permute-start | bytes 983048 | tf_op jit(solution)/shard_map/ppermute | solution.py:325
  48.0 14.2 %all-to-all-start.1 = ((f32[4,160,128]{2,1,0:T(8,128)}), f32[4,160,128]{2,1,0:T(8,128)S(1)}, u32[]{:S(2)}, u32[]{:S(2)}) async-start(f32[4,160,128]{2,1,0:T(8,128)} %bitcast.3), calls=%async_computation.1 | async-start | bytes 655360 | tf_op jit(solution)/shard_map/all_to_all | solution.py:315
  51.5 34.6 %collective-permute-start.2 = (f32[192,512]{1,0:T(8,128)S(1)}, f32[192,512]{1,0:T(8,128)S(1)}, u32[]{:S(2)}, u32[]{:S(2)}) collective-permute-start(f32[192,512]{1,0:T(8,128)S(1)} %reduce_sum.36.images_ref.refs_8_), channel_id=1, source_target_pairs={{0,2},{2,4},{4,6},{6,0},{1,3},{3,5},{5,7},{7,1},{8,10},{10,12},{12... | collective-permute-start | bytes 1179656 | tf_op jit(solution)/shard_map/ppermute | solution.py:325
  54.8 31.3 %collective-permute-start.3 = (f32[192,512]{1,0:T(8,128)S(1)}, f32[192,512]{1,0:T(8,128)S(1)}, u32[]{:S(2)}, u32[]{:S(2)}) collective-permute-start(f32[192,512]{1,0:T(8,128)S(1)} %reduce_sum.36.images_ref.refs_8_), channel_id=1, source_target_pairs={{0,4},{2,6},{4,0},{6,2},{1,5},{3,7},{5,1},{7,3},{8,12},{10,14},{12... | collective-permute-start | bytes 1179656 | tf_op jit(solution)/shard_map/ppermute | solution.py:325
  59.1 27.0 %collective-permute-start.4 = (f32[192,512]{1,0:T(8,128)S(1)}, f32[192,512]{1,0:T(8,128)S(1)}, u32[]{:S(2)}, u32[]{:S(2)}) collective-permute-start(f32[192,512]{1,0:T(8,128)S(1)} %reduce_sum.36.images_ref.refs_8_), channel_id=1, source_target_pairs={{0,6},{2,0},{4,2},{6,4},{1,7},{3,1},{5,3},{7,5},{8,14},{10,8},{12,... | collective-permute-start | bytes 1179656 | tf_op jit(solution)/shard_map/ppermute | solution.py:325
  87.3 10.2 %collective-permute-start.9 = (f32[768,512]{1,0:T(8,128)}, f32[768,512]{1,0:T(8,128)S(1)}, u32[]{:S(2)}, u32[]{:S(2)}) collective-permute-start(f32[768,512]{1,0:T(8,128)} %pad_maximum_fusion), channel_id=1, source_target_pairs={{0,1},{1,0},{2,3},{3,2},{4,5},{5,4},{6,7},{7,6},{8,9},{9,8},{10,11... | collective-permute-start | bytes 4718600 | tf_op jit(solution)/shard_map/ppermute | solution.py:325
  92.9 16.6 %all-to-all-start.3 = ((f32[64,3,128]{2,1,0:T(4,128)}), f32[64,3,128]{2,1,0:T(4,128)S(1)}, u32[]{:S(2)}, u32[]{:S(2)}) async-start(f32[64,3,128]{2,1,0:T(4,128)} %broadcast_in_dim.2), calls=%async_computation.3 | async-start | bytes 262144 | tf_op jit(solution)/shard_map/all_to_all | solution.py:315
  109.4 40.9 %all-to-all-start.4 = ((f32[64,8,512]{2,1,0:T(8,128)}), f32[64,8,512]{2,1,0:T(8,128)S(1)}, u32[]{:S(2)}, u32[]{:S(2)}) async-start(f32[64,8,512]{2,1,0:T(8,128)} %bitcast.4), calls=%async_computation.4 | async-start | bytes 2097152 | tf_op jit(solution)/shard_map/all_to_all | solution.py:315
  115.9 8.4 %collective-permute-start.5 = (f32[160,128]{1,0:T(8,128)S(1)}, f32[160,128]{1,0:T(8,128)S(1)}, u32[]{:S(2)}, u32[]{:S(2)}) collective-permute-start(f32[160,128]{1,0:T(8,128)S(1)} %slice.36.refs_0_), channel_id=1, source_target_pairs={{0,2},{2,4},{4,6},{6,0},{1,3},{3,5},{5,7},{7,1},{8,10},{10,12},{12... | collective-permute-start | bytes 245768 | tf_op jit(solution)/shard_map/ppermute | solution.py:325
  118.1 7.0 %collective-permute-start.6 = (f32[160,128]{1,0:T(8,128)S(1)}, f32[160,128]{1,0:T(8,128)S(1)}, u32[]{:S(2)}, u32[]{:S(2)}) collective-permute-start(f32[160,128]{1,0:T(8,128)S(1)} %slice.36.refs_0_), channel_id=1, source_target_pairs={{0,4},{2,6},{4,0},{6,2},{1,5},{3,7},{5,1},{7,3},{8,12},{10,14},{12... | collective-permute-start | bytes 245768 | tf_op jit(solution)/shard_map/ppermute | solution.py:325
  120.7 6.6 %collective-permute-start.7 = (f32[160,128]{1,0:T(8,128)S(1)}, f32[160,128]{1,0:T(8,128)S(1)}, u32[]{:S(2)}, u32[]{:S(2)}) collective-permute-start(f32[160,128]{1,0:T(8,128)S(1)} %slice.36.refs_0_), channel_id=1, source_target_pairs={{0,6},{2,0},{4,2},{6,4},{1,7},{3,1},{5,3},{7,5},{8,14},{10,8},{12,... | collective-permute-start | bytes 245768 | tf_op jit(solution)/shard_map/ppermute | solution.py:325
  127.3 4.6 %collective-permute-start.8 = (f32[640,128]{1,0:T(8,128)S(1)}, f32[640,128]{1,0:T(8,128)S(1)}, u32[]{:S(2)}, u32[]{:S(2)}) collective-permute-start(f32[640,128]{1,0:T(8,128)S(1)} %pad_maximum_fusion.1), channel_id=1, source_target_pairs={{0,1},{1,0},{2,3},{3,2},{4,5},{5,4},{6,7},{7,6},{8,9},{9,8},{10,11... | collective-permute-start | bytes 983048 | tf_op jit(solution)/shard_map/ppermute | solution.py:325

commit v4 on v3

--- a/solution.py
+++ b/solution.py
@@ -183,7 +183,7 @@
     )(place, *([archive] * len(images)), *images)
 
 
-def factor_block(rows):
+def factor_block(rows, spread_ref):
     shape = rows[0].shape
     lane = lax.broadcasted_iota(jnp.int32, shape, 1)
     sub = lax.broadcasted_iota(jnp.int32, shape, 0)
@@ -204,30 +204,49 @@
             panel, base = rows[p], 8 * p
             own = (lane >= base) & (lane < base + 8)
             columns = [column(panel, base + j) for j in range(8)]
-            small = [[row(columns[k], i) for k in range(i + 1)] for i in range(8)]
-            across = [
-                jnp.where(lane == base + j, 1.0, jnp.where(own, 0.0, row(panel, j))) for j in range(8)
-            ]
+            side = p % 2
+            for k, slab in enumerate([*columns, jnp.where(own, (lane == base + sub).astype(F32), panel)]):
+                spread_ref[side, 8 * k : 8 * k + 8, :] = slab
+
+            def spread(k, i):
+                return jnp.broadcast_to(spread_ref[side, 8 * k + i : 8 * k + i + 1, :], shape)
+
+            small = [[spread(k, i) for k in range(i + 1)] for i in range(8)]
+            across = [spread(8, j) for j in range(8)]
             later = range(p + 1, reach)
             down = {i: [column(rows[i], base + j) for j in range(8)] for i in later}
             for i in later:
                 rows[i] = jnp.where(own, 0.0, rows[i])
             kept = jnp.zeros(shape, F32)
             pivots = jnp.zeros(shape, F32)
-            for j in range(8):
-                inverse = 1.0 / small[j][j]
-                ratio = {i: small[i][j] * inverse for i in range(j + 1, 8)}
-                for i in range(j + 1, 8):
-                    for k in range(j + 1, i + 1):
-                        small[i][k] = small[i][k] - ratio[i] * small[k][j]
-                    across[i] = across[i] - ratio[i] * across[j]
-                scaled = across[j] * inverse
+            sizes = [1.0 / small[j][j] for j in range(0, 8, 2)]
+            for j in range(0, 8, 2):
+                n, rest = j + 1, range(j + 2, 8)
+                size = sizes[j // 2]
+                a, b, c = small[j][j] * size, small[n][j] * size, small[n][n]
+                determinant = a * c - b * small[n][j]
+                inverse = 1.0 / determinant
+                first = {i: (c * (small[i][j] * size) - b * small[i][n]) * inverse for i in rest}
+                second = {i: (a * small[i][n] - b * small[i][j]) * inverse for i in rest}
+                for i in rest:
+                    for k in range(j + 2, i + 1):
+                        change = first[i] * small[k][j] + second[i] * small[k][n]
+                        small[i][k] = small[i][k] - change
+                for i in rest:
+                    across[i] = across[i] - (first[i] * across[j] + second[i] * across[n])
+                mixed = b * inverse
+                upper = (c * inverse) * size * across[j] - mixed * across[n]
+                under = (a * inverse) * across[n] - mixed * across[j]
                 for i in later:
-                    for k in range(j + 1, 8):
-                        down[i][k] = down[i][k] - down[i][j] * ratio[k]
-                    rows[i] = rows[i] - down[i][j] * scaled
+                    for k in rest:
+                        change = down[i][j] * first[k] + down[i][n] * second[k]
+                        down[i][k] = down[i][k] - change
+                    rows[i] = rows[i] - (down[i][j] * upper + down[i][n] * under)
+                reciprocal = 1.0 / a
                 kept = jnp.where(sub == j, across[j], kept)
+                kept = jnp.where(sub == n, across[n] - (b * reciprocal) * across[j], kept)
                 pivots = jnp.where(sub == j, small[j][j], pivots)
+                pivots = jnp.where(sub == n, determinant * reciprocal, pivots)
             finished.append(kept * lax.rsqrt(pivots))
         lower = [lane <= sub + 8 * p for p in range(group, end)]
         result += [jnp.where(keep, slab, 0.0) for keep, slab in zip(lower, finished)]
@@ -245,7 +264,7 @@
 
 def factor_kernel(scale, groups, place_ref, images_ref, *refs):
     gram_refs = refs[: 2 * groups]
-    inverse_ref, basis_ref, packed_ref, work_ref = refs[2 * groups :]
+    inverse_ref, basis_ref, packed_ref, work_ref, spread_ref = refs[2 * groups :]
     size = work_ref.shape[0]
     slab = gram_refs[0].shape[0]
     for flip in range(CORES):
@@ -267,7 +286,7 @@
     diagonal = packed_ref[:BLOCK, :]
     for first in range(0, size, BLOCK):
         end = first + BLOCK
-        slabs = factor_block([diagonal[8 * i : 8 * i + 8] for i in range(BLOCK // 8)])
+        slabs = factor_block([diagonal[8 * i : 8 * i + 8] for i in range(BLOCK // 8)], spread_ref)
         work_ref[first:end, first:end] = unit
         panel = six_pass_dot(jnp.concatenate(slabs, 0), work_ref[first:end, :], 1, 0)
         finished = panel[:, :end]
@@ -298,6 +317,7 @@
             scratch_shapes=[
                 pltpu.VMEM((len(upper_blocks(size)) * BLOCK, BLOCK), F32),
                 pltpu.VMEM((size, size), F32),
+                pltpu.VMEM((2, 72, BLOCK), F32),
             ],
         ),
         out_shape=[

time: 153 us -> 150 us (0.980)
  Pallas kernels: 31 us -> 28.2 us
    pallas_call x1, Pallas kernels: 18.4 us -> 15.6 us  [factor(): pl.pallas_call(functools.partial(factor_kernel, scale, len(pieces) // COR...]
  transfers between devices with their start and end apart: 13 -> 13, of which waited for: 6 -> 6; matrix products, arithmetic and copies ran while one was open for 1% -> 1% of each run, Pallas kernels for 18% -> 16%
where the time goes in v4:
time: 150 us; the launch traced here: 149 us
  starting transfers between devices  53.9 us (36%)
  blocking collectives  46.6 us (31%)
  Pallas kernels  28.2 us (19%)
  waiting for transfers between devices  11.2 us (7%)
  local copies, waits for them, and re-layouts  4.04 us (3%)
  other arithmetic  2.85 us (2%)
  matrix products  1.58 us (1%)
    all_to_all x2, blocking collectives, exchange(): return lax.all_to_all(blocks, axes, 0, 0, tiled=True)  46.6 us
    ppermute x10, starting transfers between devices, shifted(): lax.ppermute(block, axis, [(i, (i + by) % size) for i in range(size)])  39.4 us
    pallas_call x1, Pallas kernels, factor(): pl.pallas_call(functools.partial(factor_kernel, scale, len(pieces) // COR...  15.6 us
    all_to_all x3, starting transfers between devices, exchange(): return lax.all_to_all(blocks, axes, 0, 0, tiled=True)  14.4 us
    pallas_call x1, Pallas kernels, moved_rows(): pl.pallas_call(functools.partial(moved_kernel, len(images)), grid_spec=pl...  6.03 us
    all_to_all x3, waiting for transfers between devices, exchange(): return lax.all_to_all(blocks, axes, 0, 0, tiled=True)  5.77 us
    pallas_call x2, Pallas kernels, partial_images(): pl.pallas_call(images_kernel, grid_spec=pltpu.PrefetchScalarGridSpec(num_...  5.56 us
    ppermute x10, waiting for transfers between devices, shifted(): lax.ppermute(block, axis, [(i, (i + by) % size) for i in range(size)])  5.45 us
  transfers between devices with their start and end apart: 13, of which 6 were waited for; matrix products, arithmetic and copies ran while one was open for 1% of the time, Pallas kernels for 16%

profile of v4, /device:TPU:1, one launch (start us, length us, event | category | flops | bytes accessed | tf_op | source)
XLA Modules:
  0.0 149.2 jit_solution(9731846949502318843)
XLA Ops:
  0.7 1.9 %copy-done = f32[1536,512]{1,0:T(8,128)S(1)} copy-done((f32[1536,512]{1,0:T(8,128)S(1)}, f32[1536,512]{1,0:T(8,128)}, u32[]{:S(2)}) %copy-start) | copy-done | bytes 3145752
  2.6 1.2 copy-done.1
  3.8 2.8 %shard_map.42 = f32[768,512]{1,0:T(8,128)S(1)} custom-call(s32[2]{0:T(128)S(1)} %pad_add_fusion.place_ref, f32[1536,512]{1,0:T(8,128)S(1)} %copy-done, f32[512,512]{1,0:T(8,128)S(1)} %copy-done.1), custom_call_target="tpu_custom_call" | custom-call | flops 1207959552 | bytes 6291456 | tf_op jit(solution)/shard_map/pallas_call | solution.py:82
  6.6 8.8 %collective-permute-start = (f32[768,512]{1,0:T(8,128)S(1)}, f32[768,512]{1,0:T(8,128)S(1)}, u32[]{:S(2)}, u32[]{:S(2)}) collective-permute-start(f32[768,512]{1,0:T(8,128)S(1)} %shard_map.42), channel_id=1, source_target_pairs={{0,1},{1,0},{2,3},{3,2},{4,5},{5,4},{6,7},{7,6},{8,9},{9,8},{10,11... | collective-permute-start | bytes 4718600 | tf_op jit(solution)/shard_map/ppermute | solution.py:345
  15.4 2.8 %shard_map.41 = f32[768,512]{1,0:T(8,128)S(1)} custom-call(s32[2]{0:T(128)S(1)} %pad_add_fusion.place_ref, f32[1536,512]{1,0:T(8,128)S(1)} %copy-done, f32[512,512]{1,0:T(8,128)S(1)} %copy-done.1), custom_call_target="tpu_custom_call" | custom-call | flops 1207959552 | bytes 6291456 | tf_op jit(solution)/shard_map/pallas_call | solution.py:82
  18.4 0.3 add.8
  18.8 22.9 %all_to_all.25 = f32[4,192,512]{2,1,0:T(8,128)S(1)} all-to-all(f32[4,192,512]{2,1,0:T(8,128)S(1)} %bitcast.7), channel_id=1, replica_groups=mesh['z'=8,'y'=8,'x'=4,'core'=2] {'x'}, dimensions={0} | all-to-all | bytes 3145728 | tf_op jit(solution)/shard_map/all_to_all | solution.py:335
  41.9 1.0 shard_map.43
  42.9 3.1 %collective-permute-start.1 = (f32[640,128]{1,0:T(8,128)S(1)}, f32[640,128]{1,0:T(8,128)S(1)}, u32[]{:S(2)}, u32[]{:S(2)}) collective-permute-start(f32[640,128]{1,0:T(8,128)S(1)} %get-tuple-element.12), channel_id=1, source_target_pairs={{0,1},{1,0},{2,3},{3,2},{4,5},{5,4},{6,7},{7,6},{8,9},{9,8},{10,11... | collective-permute-start | bytes 983048 | tf_op jit(solution)/shard_map/ppermute | solution.py:345
  46.0 1.2 collective-permute-done.1
  47.2 0.8 add.9
  48.0 3.5 %all-to-all-start.1 = ((f32[4,160,128]{2,1,0:T(8,128)}), f32[4,160,128]{2,1,0:T(8,128)S(1)}, u32[]{:S(2)}, u32[]{:S(2)}) async-start(f32[4,160,128]{2,1,0:T(8,128)} %bitcast.3), calls=%async_computation.1 | async-start | bytes 655360 | tf_op jit(solution)/shard_map/all_to_all | solution.py:335
  51.5 3.3 %collective-permute-start.2 = (f32[192,512]{1,0:T(8,128)S(1)}, f32[192,512]{1,0:T(8,128)S(1)}, u32[]{:S(2)}, u32[]{:S(2)}) collective-permute-start(f32[192,512]{1,0:T(8,128)S(1)} %reduce_sum.36.images_ref.refs_8_), channel_id=1, source_target_pairs={{0,2},{2,4},{4,6},{6,0},{1,3},{3,5},{5,7},{7,1},{8,10},{10,12},{12... | collective-permute-start | bytes 1179656 | tf_op jit(solution)/shard_map/ppermute | solution.py:345
  54.8 4.3 %collective-permute-start.3 = (f32[192,512]{1,0:T(8,128)S(1)}, f32[192,512]{1,0:T(8,128)S(1)}, u32[]{:S(2)}, u32[]{:S(2)}) collective-permute-start(f32[192,512]{1,0:T(8,128)S(1)} %reduce_sum.36.images_ref.refs_8_), channel_id=1, source_target_pairs={{0,4},{2,6},{4,0},{6,2},{1,5},{3,7},{5,1},{7,3},{8,12},{10,14},{12... | collective-permute-start | bytes 1179656 | tf_op jit(solution)/shard_map/ppermute | solution.py:345
  59.1 3.1 %collective-permute-start.4 = (f32[192,512]{1,0:T(8,128)S(1)}, f32[192,512]{1,0:T(8,128)S(1)}, u32[]{:S(2)}, u32[]{:S(2)}) collective-permute-start(f32[192,512]{1,0:T(8,128)S(1)} %reduce_sum.36.images_ref.refs_8_), channel_id=1, source_target_pairs={{0,6},{2,0},{4,2},{6,4},{1,7},{3,1},{5,3},{7,5},{8,14},{10,8},{12,... | collective-permute-start | bytes 1179656 | tf_op jit(solution)/shard_map/ppermute | solution.py:345
  62.3 23.7 %all_to_all.26 = f32[64,3,128]{2,1,0:T(4,128)S(1)} all-to-all(f32[64,3,128]{2,1,0:T(4,128)S(1)} %reshape.22), channel_id=1, replica_groups=mesh['z'=8,'y'=8,'x'=4,'core'=2] {'z','y'}, dimensions={0} | all-to-all | bytes 196608 | tf_op jit(solution)/shard_map/all_to_all | solution.py:335
  86.1 1.3 pad_maximum_fusion
  87.3 4.9 %collective-permute-start.9 = (f32[768,512]{1,0:T(8,128)}, f32[768,512]{1,0:T(8,128)S(1)}, u32[]{:S(2)}, u32[]{:S(2)}) collective-permute-start(f32[768,512]{1,0:T(8,128)} %pad_maximum_fusion), channel_id=1, source_target_pairs={{0,1},{1,0},{2,3},{3,2},{4,5},{5,4},{6,7},{7,6},{8,9},{9,8},{10,11... | collective-permute-start | bytes 4718600 | tf_op jit(solution)/shard_map/ppermute | solution.py:345
  92.2 0.7 broadcast_in_dim.2
  92.9 4.6 %all-to-all-start.3 = ((f32[64,3,128]{2,1,0:T(4,128)}), f32[64,3,128]{2,1,0:T(4,128)S(1)}, u32[]{:S(2)}, u32[]{:S(2)}) async-start(f32[64,3,128]{2,1,0:T(4,128)} %broadcast_in_dim.2), calls=%async_computation.3 | async-start | bytes 262144 | tf_op jit(solution)/shard_map/all_to_all | solution.py:335
  97.6 6.0 %shard_map.45 = f32[512,512]{1,0:T(8,128)} custom-call(s32[2]{0:T(128)S(1)} %pad_add_fusion.place_ref, f32[1536,512]{1,0:T(8,128)} %refs_7_.1, f32[1536,512]{1,0:T(8,128)} %refs_7_.1, f32[1536,512]{1,0:T(8,128)} %refs_7_.1, f32[1536,512]{1,0:T(8,128)} %refs_7_.1, f32[1536,512]{1,0:T(8,128)} %refs_7_.1, f32[1536,512]{1,0:T(8,128)} %refs_7_.1, ...), custom_call_target="tpu_custom_call" | custom-call | flops 2415919104 | bytes 6291456 | tf_op jit(solution)/shard_map/pallas_call | solution.py:169
  103.7 5.8 %all-to-all-done.3 = f32[64,3,128]{2,1,0:T(4,128)S(1)} async-done(((f32[64,3,128]{2,1,0:T(4,128)}), f32[64,3,128]{2,1,0:T(4,128)S(1)}, u32[]{:S(2)}, u32[]{:S(2)}) %all-to-all-start.3) | async-done | bytes 98336 | tf_op jit(solution)/shard_map/all_to_all | solution.py:335
  109.4 6.4 %all-to-all-start.4 = ((f32[64,8,512]{2,1,0:T(8,128)}), f32[64,8,512]{2,1,0:T(8,128)S(1)}, u32[]{:S(2)}, u32[]{:S(2)}) async-start(f32[64,8,512]{2,1,0:T(8,128)} %bitcast.4), calls=%async_computation.4 | async-start | bytes 2097152 | tf_op jit(solution)/shard_map/all_to_all | solution.py:335
  115.9 2.2 %collective-permute-start.5 = (f32[160,128]{1,0:T(8,128)S(1)}, f32[160,128]{1,0:T(8,128)S(1)}, u32[]{:S(2)}, u32[]{:S(2)}) collective-permute-start(f32[160,128]{1,0:T(8,128)S(1)} %slice.36.refs_0_), channel_id=1, source_target_pairs={{0,2},{2,4},{4,6},{6,0},{1,3},{3,5},{5,7},{7,1},{8,10},{10,12},{12... | collective-permute-start | bytes 245768 | tf_op jit(solution)/shard_map/ppermute | solution.py:345
  118.1 2.5 %collective-permute-start.6 = (f32[160,128]{1,0:T(8,128)S(1)}, f32[160,128]{1,0:T(8,128)S(1)}, u32[]{:S(2)}, u32[]{:S(2)}) collective-permute-start(f32[160,128]{1,0:T(8,128)S(1)} %slice.36.refs_0_), channel_id=1, source_target_pairs={{0,4},{2,6},{4,0},{6,2},{1,5},{3,7},{5,1},{7,3},{8,12},{10,14},{12... | collective-permute-start | bytes 245768 | tf_op jit(solution)/shard_map/ppermute | solution.py:345
  120.7 3.7 %collective-permute-start.7 = (f32[160,128]{1,0:T(8,128)S(1)}, f32[160,128]{1,0:T(8,128)S(1)}, u32[]{:S(2)}, u32[]{:S(2)}) collective-permute-start(f32[160,128]{1,0:T(8,128)S(1)} %slice.36.refs_0_), channel_id=1, source_target_pairs={{0,6},{2,0},{4,2},{6,4},{1,7},{3,1},{5,3},{7,5},{8,14},{10,8},{12,... | collective-permute-start | bytes 245768 | tf_op jit(solution)/shard_map/ppermute | solution.py:345
  124.3 0.7 collective-permute-done.6.refs_2_
  125.1 2.2 %collective-permute-done.7.refs_3_ = f32[160,128]{1,0:T(8,128)S(1)} collective-permute-done((f32[160,128]{1,0:T(8,128)S(1)}, f32[160,128]{1,0:T(8,128)S(1)}, u32[]{:S(2)}, u32[]{:S(2)}) %collective-permute-start.7) | collective-permute-done | bytes 81952 | tf_op jit(solution)/shard_map/ppermute | solution.py:345
  127.3 3.5 %collective-permute-start.8 = (f32[640,128]{1,0:T(8,128)S(1)}, f32[640,128]{1,0:T(8,128)S(1)}, u32[]{:S(2)}, u32[]{:S(2)}) collective-permute-start(f32[640,128]{1,0:T(8,128)S(1)} %pad_maximum_fusion.1), channel_id=1, source_target_pairs={{0,1},{1,0},{2,3},{3,2},{4,5},{5,4},{6,7},{7,6},{8,9},{9,8},{10,11... | collective-permute-start | bytes 983048 | tf_op jit(solution)/shard_map/ppermute | solution.py:345
  130.8 1.1 collective-permute-done.8
  131.9 15.6 %shard_map.44 = (f32[512,512]{1,0:T(8,128)S(1)}, f32[192,512]{1,0:T(8,128)}) custom-call(s32[2]{0:T(128)S(1)} %pad_add_fusion.place_ref, f32[192,512]{1,0:T(8,128)S(1)} %reduce_sum.36.images_ref.refs_8_, f32[160,128]{1,0:T(8,128)S(1)} %slice.36.refs_0_, f32[160,128]{1,0:T(8,128)S(1)} %collective-permute-done.5.refs_1_, ...), custom_call_target="tpu_custom_call" | custom-call | flops 524288 | bytes 512 | tf_op jit(solution)/shard_map/pallas_call | solution.py:310
  147.6 1.6 %fusion.2 = f32[8,512]{1,0:T(8,128)} fusion(f32[8,512]{1,0:T(8,128)S(1)} %reduce_sum.39, f32[512,512]{1,0:T(8,128)S(1)} %get-tuple-element.19), kind=kOutput, calls=%fused_computation.5 | convolution fusion | flops 25165824 | bytes 1081344 | tf_op jit(solution)/shard_map/dot_general | solution.py:23
  (22 shorter events, 1.0 us)
Async XLA Ops:
  0.7 1.9 %copy-start = (f32[1536,512]{1,0:T(8,128)S(1)}, f32[1536,512]{1,0:T(8,128)}, u32[]{:S(2)}) copy-start(f32[1536,512]{1,0:T(8,128)} %refs_7_.1) | copy-start | bytes 9437188
  2.6 1.2 copy-start.1
  6.6 11.8 %collective-permute-start = (f32[768,512]{1,0:T(8,128)S(1)}, f32[768,512]{1,0:T(8,128)S(1)}, u32[]{:S(2)}, u32[]{:S(2)}) collective-permute-start(f32[768,512]{1,0:T(8,128)S(1)} %shard_map.42), channel_id=1, source_target_pairs={{0,1},{1,0},{2,3},{3,2},{4,5},{5,4},{6,7},{7,6},{8,9},{9,8},{10,11... | collective-permute-start | bytes 4718600 | tf_op jit(solution)/shard_map/ppermute | solution.py:345
  42.9 4.4 %collective-permute-start.1 = (f32[640,128]{1,0:T(8,128)S(1)}, f32[640,128]{1,0:T(8,128)S(1)}, u32[]{:S(2)}, u32[]{:S(2)}) collective-permute-start(f32[640,128]{1,0:T(8,128)S(1)} %get-tuple-element.12), channel_id=1, source_target_pairs={{0,1},{1,0},{2,3},{3,2},{4,5},{5,4},{6,7},{7,6},{8,9},{9,8},{10,11... | collective-permute-start | bytes 983048 | tf_op jit(solution)/shard_map/ppermute | solution.py:345
  48.0 14.2 %all-to-all-start.1 = ((f32[4,160,128]{2,1,0:T(8,128)}), f32[4,160,128]{2,1,0:T(8,128)S(1)}, u32[]{:S(2)}, u32[]{:S(2)}) async-start(f32[4,160,128]{2,1,0:T(8,128)} %bitcast.3), calls=%async_computation.1 | async-start | bytes 655360 | tf_op jit(solution)/shard_map/all_to_all | solution.py:335
  51.5 34.6 %collective-permute-start.2 = (f32[192,512]{1,0:T(8,128)S(1)}, f32[192,512]{1,0:T(8,128)S(1)}, u32[]{:S(2)}, u32[]{:S(2)}) collective-permute-start(f32[192,512]{1,0:T(8,128)S(1)} %reduce_sum.36.images_ref.refs_8_), channel_id=1, source_target_pairs={{0,2},{2,4},{4,6},{6,0},{1,3},{3,5},{5,7},{7,1},{8,10},{10,12},{12... | collective-permute-start | bytes 1179656 | tf_op jit(solution)/shard_map/ppermute | solution.py:345
  54.8 31.3 %collective-permute-start.3 = (f32[192,512]{1,0:T(8,128)S(1)}, f32[192,512]{1,0:T(8,128)S(1)}, u32[]{:S(2)}, u32[]{:S(2)}) collective-permute-start(f32[192,512]{1,0:T(8,128)S(1)} %reduce_sum.36.images_ref.refs_8_), channel_id=1, source_target_pairs={{0,4},{2,6},{4,0},{6,2},{1,5},{3,7},{5,1},{7,3},{8,12},{10,14},{12... | collective-permute-start | bytes 1179656 | tf_op jit(solution)/shard_map/ppermute | solution.py:345
  59.1 27.0 %collective-permute-start.4 = (f32[192,512]{1,0:T(8,128)S(1)}, f32[192,512]{1,0:T(8,128)S(1)}, u32[]{:S(2)}, u32[]{:S(2)}) collective-permute-start(f32[192,512]{1,0:T(8,128)S(1)} %reduce_sum.36.images_ref.refs_8_), channel_id=1, source_target_pairs={{0,6},{2,0},{4,2},{6,4},{1,7},{3,1},{5,3},{7,5},{8,14},{10,8},{12,... | collective-permute-start | bytes 1179656 | tf_op jit(solution)/shard_map/ppermute | solution.py:345
  87.3 10.2 %collective-permute-start.9 = (f32[768,512]{1,0:T(8,128)}, f32[768,512]{1,0:T(8,128)S(1)}, u32[]{:S(2)}, u32[]{:S(2)}) collective-permute-start(f32[768,512]{1,0:T(8,128)} %pad_maximum_fusion), channel_id=1, source_target_pairs={{0,1},{1,0},{2,3},{3,2},{4,5},{5,4},{6,7},{7,6},{8,9},{9,8},{10,11... | collective-permute-start | bytes 4718600 | tf_op jit(solution)/shard_map/ppermute | solution.py:345
  92.9 16.6 %all-to-all-start.3 = ((f32[64,3,128]{2,1,0:T(4,128)}), f32[64,3,128]{2,1,0:T(4,128)S(1)}, u32[]{:S(2)}, u32[]{:S(2)}) async-start(f32[64,3,128]{2,1,0:T(4,128)} %broadcast_in_dim.2), calls=%async_computation.3 | async-start | bytes 262144 | tf_op jit(solution)/shard_map/all_to_all | solution.py:335
  109.4 38.1 %all-to-all-start.4 = ((f32[64,8,512]{2,1,0:T(8,128)}), f32[64,8,512]{2,1,0:T(8,128)S(1)}, u32[]{:S(2)}, u32[]{:S(2)}) async-start(f32[64,8,512]{2,1,0:T(8,128)} %bitcast.4), calls=%async_computation.4 | async-start | bytes 2097152 | tf_op jit(solution)/shard_map/all_to_all | solution.py:335
  115.9 8.4 %collective-permute-start.5 = (f32[160,128]{1,0:T(8,128)S(1)}, f32[160,128]{1,0:T(8,128)S(1)}, u32[]{:S(2)}, u32[]{:S(2)}) collective-permute-start(f32[160,128]{1,0:T(8,128)S(1)} %slice.36.refs_0_), channel_id=1, source_target_pairs={{0,2},{2,4},{4,6},{6,0},{1,3},{3,5},{5,7},{7,1},{8,10},{10,12},{12... | collective-permute-start | bytes 245768 | tf_op jit(solution)/shard_map/ppermute | solution.py:345
  118.1 7.0 %collective-permute-start.6 = (f32[160,128]{1,0:T(8,128)S(1)}, f32[160,128]{1,0:T(8,128)S(1)}, u32[]{:S(2)}, u32[]{:S(2)}) collective-permute-start(f32[160,128]{1,0:T(8,128)S(1)} %slice.36.refs_0_), channel_id=1, source_target_pairs={{0,4},{2,6},{4,0},{6,2},{1,5},{3,7},{5,1},{7,3},{8,12},{10,14},{12... | collective-permute-start | bytes 245768 | tf_op jit(solution)/shard_map/ppermute | solution.py:345
  120.7 6.6 %collective-permute-start.7 = (f32[160,128]{1,0:T(8,128)S(1)}, f32[160,128]{1,0:T(8,128)S(1)}, u32[]{:S(2)}, u32[]{:S(2)}) collective-permute-start(f32[160,128]{1,0:T(8,128)S(1)} %slice.36.refs_0_), channel_id=1, source_target_pairs={{0,6},{2,0},{4,2},{6,4},{1,7},{3,1},{5,3},{7,5},{8,14},{10,8},{12,... | collective-permute-start | bytes 245768 | tf_op jit(solution)/shard_map/ppermute | solution.py:345
  127.3 4.6 %collective-permute-start.8 = (f32[640,128]{1,0:T(8,128)S(1)}, f32[640,128]{1,0:T(8,128)S(1)}, u32[]{:S(2)}, u32[]{:S(2)}) collective-permute-start(f32[640,128]{1,0:T(8,128)S(1)} %pad_maximum_fusion.1), channel_id=1, source_target_pairs={{0,1},{1,0},{2,3},{3,2},{4,5},{5,4},{6,7},{7,6},{8,9},{9,8},{10,11... | collective-permute-start | bytes 983048 | tf_op jit(solution)/shard_map/ppermute | solution.py:345

commit v5 on v4

--- a/solution.py
+++ b/solution.py
@@ -59,7 +59,7 @@
     return device * CORES + (1 - place[0] if flip else place[0])
 
 
-def images_kernel(place_ref, archive_ref, sketch_ref, out_ref, sketch_halves):
+def images_kernel(place_ref, first_ref, second_ref, sketch_ref, out_ref, sketch_halves):
     depth = sketch_ref.shape[0]
 
     @pl.when(pl.program_id(0) == 0)
@@ -69,7 +69,7 @@
         sketch_halves[depth : 2 * depth] = high
         sketch_halves[2 * depth :] = low
 
-    high, low = halves(archive_ref[...])
+    high, low = halves(jnp.concatenate([first_ref[...], second_ref[...]], 0))
     out_ref[...] = jnp.dot(
         jnp.concatenate([high, low, high], 1), sketch_halves[...], preferred_element_type=F32
     )
@@ -83,12 +83,13 @@
         images_kernel,
         grid_spec=pltpu.PrefetchScalarGridSpec(
             num_scalar_prefetch=1,
-            grid=(groups,),
+            grid=(groups // 2,),
             in_specs=[
-                pl.BlockSpec((block, depth), lambda i, place: (row_block(place, i, flip), 0)),
+                pl.BlockSpec((block, depth), lambda i, place: (row_block(place, 2 * i, flip), 0)),
+                pl.BlockSpec((block, depth), lambda i, place: (row_block(place, 2 * i + 1, flip), 0)),
                 pl.BlockSpec((depth, width), lambda i, place: (0, 0)),
             ],
-            out_specs=pl.BlockSpec((block, width), lambda i, place: (i, 0)),
+            out_specs=pl.BlockSpec((2 * block, width), lambda i, place: (i, 0)),
             scratch_shapes=[pltpu.VMEM((3 * depth, width), BF16)],
         ),
         out_shape=jax.ShapeDtypeStruct((groups * block, width), F32),
@@ -96,7 +97,7 @@
         cost_estimate=pl.CostEstimate(
             flops=3 * rows * depth * width, bytes_accessed=8 * rows * depth, transcendentals=0
         ),
-    )(place, archive, sketch)
+    )(place, archive, archive, sketch)
 
 
 def whole(shape):
@@ -364,9 +365,11 @@
     kept, sent = gram_halves(own, place)
     gram = kept + shifted(sent, "core", 1)
     gram = exchange(gram.reshape(groups, slab_rows, BLOCK), "x").sum(0)
-    per = pl.cdiv(slab_rows, stacked)
-    split = jnp.pad(gram, ((0, per * stacked - slab_rows), (0, 0))).reshape(stacked, per, BLOCK)
-    row = exchange(split, over_rows).sum(0)
+    across = lax.axis_size("y")
+    per = pl.cdiv(slab_rows, across * 8) * 8
+    split = jnp.pad(gram, ((0, per * across - slab_rows), (0, 0))).reshape(across, per, BLOCK)
+    row = exchange(split, "y").sum(0)
+    row = gather(row, "z").sum(0)
 
     near = [own, *(shifted(own, "x", s) for s in range(1, groups))]
     row, near = lax.optimization_barrier((row, near))
@@ -374,7 +377,7 @@
     far = [far[s * own_rows : (s + 1) * own_rows] for s in range(groups)]
     moved = moved_rows(archive, near, far, place, groups)
 
-    gram = gather(row, over_rows).reshape(per * stacked, BLOCK)[:slab_rows]
+    gram = gather(row, "y").reshape(per * across, BLOCK)[:slab_rows]
     moved = exchange(moved.reshape(stacked, -1, width), over_rows)
     here = [gram, *(shifted(gram, "x", s) for s in range(1, groups))]
     there = shifted(jnp.concatenate(here, 0), "core", 1)

time: 150 us -> 149 us (level)
  blocking collectives: 46.6 us -> 50.7 us
  waiting for transfers between devices: 11.2 us -> 7.73 us
    all_to_all x2 -> x3, blocking collectives: 46.6 us -> 50.7 us  [exchange(): return lax.all_to_all(blocks, axes, 0, 0, tiled=True)]
    all_to_all x3, waiting for transfers between devices: 5.77 us -> 1.83 us  [exchange(): return lax.all_to_all(blocks, axes, 0, 0, tiled=True)]
    all_to_all x3, starting transfers between devices: 14.4 us -> 12.6 us  [exchange(): return lax.all_to_all(blocks, axes, 0, 0, tiled=True)]
where the time goes in v5:
time: 149 us; the launch traced here: 148 us
  starting transfers between devices  53.2 us (36%)
  blocking collectives  50.7 us (34%)
  Pallas kernels  27.3 us (18%)
  waiting for transfers between devices  7.73 us (5%)
  local copies, waits for them, and re-layouts  3.93 us (3%)
  other arithmetic  2.79 us (2%)
  matrix products  1.58 us (1%)
    all_to_all x3, blocking collectives, exchange(): return lax.all_to_all(blocks, axes, 0, 0, tiled=True)  50.7 us
    ppermute x10, starting transfers between devices, shifted(): lax.ppermute(block, axis, [(i, (i + by) % size) for i in range(size)])  40.7 us
    pallas_call x1, Pallas kernels, factor(): pl.pallas_call(functools.partial(factor_kernel, scale, len(pieces) // COR...  15.6 us
    all_to_all x3, starting transfers between devices, exchange(): return lax.all_to_all(blocks, axes, 0, 0, tiled=True)  12.6 us
    pallas_call x1, Pallas kernels, moved_rows(): pl.pallas_call(functools.partial(moved_kernel, len(images)), grid_spec=pl...  6.02 us
    ppermute x10, waiting for transfers between devices, shifted(): lax.ppermute(block, axis, [(i, (i + by) % size) for i in range(size)])  5.9 us
    pallas_call x2, Pallas kernels, partial_images(): pl.pallas_call(images_kernel, grid_spec=pltpu.PrefetchScalarGridSpec(num_...  4.66 us
    unnamed x4, local copies, waits for them, and re-layouts  3.11 us
  transfers between devices with their start and end apart: 13, of which 6 were waited for; matrix products, arithmetic and copies ran while one was open for 1% of the time, Pallas kernels for 16%

profile of v5, /device:TPU:1, one launch (start us, length us, event | category | flops | bytes accessed | tf_op | source)
XLA Modules:
  0.0 148.1 jit_solution(14895770645530715789)
XLA Ops:
  0.7 1.9 %copy-done = f32[1536,512]{1,0:T(8,128)S(1)} copy-done((f32[1536,512]{1,0:T(8,128)S(1)}, f32[1536,512]{1,0:T(8,128)}, u32[]{:S(2)}) %copy-start) | copy-done | bytes 3145752
  2.6 1.2 copy-done.1
  3.8 2.3 %shard_map.42 = f32[768,512]{1,0:T(8,128)S(1)} custom-call(s32[2]{0:T(128)S(1)} %pad_add_fusion.place_ref, f32[1536,512]{1,0:T(8,128)S(1)} %copy-done, f32[1536,512]{1,0:T(8,128)S(1)} %copy-done, f32[512,512]{1,0:T(8,128)S(1)} %copy-done.1), custom_call_target="tpu_custom_call" | custom-call | flops 1207959552 | bytes 6291456 | tf_op jit(solution)/shard_map/pallas_call | solution.py:82
  6.2 8.8 %collective-permute-start = (f32[768,512]{1,0:T(8,128)S(1)}, f32[768,512]{1,0:T(8,128)S(1)}, u32[]{:S(2)}, u32[]{:S(2)}) collective-permute-start(f32[768,512]{1,0:T(8,128)S(1)} %shard_map.42), channel_id=1, source_target_pairs={{0,1},{1,0},{2,3},{3,2},{4,5},{5,4},{6,7},{7,6},{8,9},{9,8},{10,11... | collective-permute-start | bytes 4718600 | tf_op jit(solution)/shard_map/ppermute | solution.py:346
  15.0 2.3 %shard_map.41 = f32[768,512]{1,0:T(8,128)S(1)} custom-call(s32[2]{0:T(128)S(1)} %pad_add_fusion.place_ref, f32[1536,512]{1,0:T(8,128)S(1)} %copy-done, f32[1536,512]{1,0:T(8,128)S(1)} %copy-done, f32[512,512]{1,0:T(8,128)S(1)} %copy-done.1), custom_call_target="tpu_custom_call" | custom-call | flops 1207959552 | bytes 6291456 | tf_op jit(solution)/shard_map/pallas_call | solution.py:82
  17.3 0.7 collective-permute-done
  18.3 22.9 %all_to_all.30 = f32[4,192,512]{2,1,0:T(8,128)S(1)} all-to-all(f32[4,192,512]{2,1,0:T(8,128)S(1)} %bitcast.9), channel_id=1, replica_groups=mesh['z'=8,'y'=8,'x'=4,'core'=2] {'x'}, dimensions={0} | all-to-all | bytes 3145728 | tf_op jit(solution)/shard_map/all_to_all | solution.py:336
  41.4 1.0 shard_map.43
  42.4 3.1 %collective-permute-start.1 = (f32[640,128]{1,0:T(8,128)S(1)}, f32[640,128]{1,0:T(8,128)S(1)}, u32[]{:S(2)}, u32[]{:S(2)}) collective-permute-start(f32[640,128]{1,0:T(8,128)S(1)} %get-tuple-element.12), channel_id=1, source_target_pairs={{0,1},{1,0},{2,3},{3,2},{4,5},{5,4},{6,7},{7,6},{8,9},{9,8},{10,11... | collective-permute-start | bytes 983048 | tf_op jit(solution)/shard_map/ppermute | solution.py:346
  45.6 1.2 collective-permute-done.1
  46.8 0.8 add.9
  47.6 3.5 %all-to-all-start.1 = ((f32[4,160,128]{2,1,0:T(8,128)}), f32[4,160,128]{2,1,0:T(8,128)S(1)}, u32[]{:S(2)}, u32[]{:S(2)}) async-start(f32[4,160,128]{2,1,0:T(8,128)} %bitcast.3), calls=%async_computation.1 | async-start | bytes 655360 | tf_op jit(solution)/shard_map/all_to_all | solution.py:336
  51.0 3.3 %collective-permute-start.2 = (f32[192,512]{1,0:T(8,128)S(1)}, f32[192,512]{1,0:T(8,128)S(1)}, u32[]{:S(2)}, u32[]{:S(2)}) collective-permute-start(f32[192,512]{1,0:T(8,128)S(1)} %reduce_sum.45.images_ref.refs_8_), channel_id=1, source_target_pairs={{0,2},{2,4},{4,6},{6,0},{1,3},{3,5},{5,7},{7,1},{8,10},{10,12},{12... | collective-permute-start | bytes 1179656 | tf_op jit(solution)/shard_map/ppermute | solution.py:346
  54.3 4.3 %collective-permute-start.3 = (f32[192,512]{1,0:T(8,128)S(1)}, f32[192,512]{1,0:T(8,128)S(1)}, u32[]{:S(2)}, u32[]{:S(2)}) collective-permute-start(f32[192,512]{1,0:T(8,128)S(1)} %reduce_sum.45.images_ref.refs_8_), channel_id=1, source_target_pairs={{0,4},{2,6},{4,0},{6,2},{1,5},{3,7},{5,1},{7,3},{8,12},{10,14},{12... | collective-permute-start | bytes 1179656 | tf_op jit(solution)/shard_map/ppermute | solution.py:346
  58.7 3.1 %collective-permute-start.4 = (f32[192,512]{1,0:T(8,128)S(1)}, f32[192,512]{1,0:T(8,128)S(1)}, u32[]{:S(2)}, u32[]{:S(2)}) collective-permute-start(f32[192,512]{1,0:T(8,128)S(1)} %reduce_sum.45.images_ref.refs_8_), channel_id=1, source_target_pairs={{0,6},{2,0},{4,2},{6,4},{1,7},{3,1},{5,3},{7,5},{8,14},{10,8},{12,... | collective-permute-start | bytes 1179656 | tf_op jit(solution)/shard_map/ppermute | solution.py:346
  61.8 10.2 %all_to_all.31 = f32[8,24,128]{2,1,0:T(8,128)S(1)} all-to-all(f32[8,24,128]{2,1,0:T(8,128)S(1)} %bitcast.10), channel_id=1, replica_groups=mesh['z'=8,'y'=8,'x'=4,'core'=2] {'y'}, dimensions={0} | all-to-all | bytes 196608 | tf_op jit(solution)/shard_map/all_to_all | solution.py:336
  72.1 17.5 %all_to_all.32 = f32[8,24,128]{2,1,0:T(8,128)S(1)} all-to-all(f32[8,24,128]{2,1,0:T(8,128)S(1)} %broadcast_in_dim.4), channel_id=1, replica_groups=mesh['z'=8,'y'=8,'x'=4,'core'=2] {'z'}, dimensions={0} | all-to-all | bytes 196608 | tf_op jit(solution)/shard_map/all_to_all | solution.py:336
  89.6 1.3 pad_maximum_fusion
  90.9 6.1 %collective-permute-start.9 = (f32[768,512]{1,0:T(8,128)}, f32[768,512]{1,0:T(8,128)S(1)}, u32[]{:S(2)}, u32[]{:S(2)}) collective-permute-start(f32[768,512]{1,0:T(8,128)} %pad_maximum_fusion), channel_id=1, source_target_pairs={{0,1},{1,0},{2,3},{3,2},{4,5},{5,4},{6,7},{7,6},{8,9},{9,8},{10,11... | collective-permute-start | bytes 4718600 | tf_op jit(solution)/shard_map/ppermute | solution.py:346
  97.7 3.4 %all-to-all-start.4 = ((f32[8,24,128]{2,1,0:T(8,128)}), f32[8,24,128]{2,1,0:T(8,128)S(1)}, u32[]{:S(2)}, u32[]{:S(2)}) async-start(f32[8,24,128]{2,1,0:T(8,128)} %broadcast_in_dim.5), calls=%async_computation.4 | async-start | bytes 196608 | tf_op jit(solution)/shard_map/all_to_all | solution.py:336
  101.2 6.0 %shard_map.45 = f32[512,512]{1,0:T(8,128)} custom-call(s32[2]{0:T(128)S(1)} %pad_add_fusion.place_ref, f32[1536,512]{1,0:T(8,128)} %refs_7_.1, f32[1536,512]{1,0:T(8,128)} %refs_7_.1, f32[1536,512]{1,0:T(8,128)} %refs_7_.1, f32[1536,512]{1,0:T(8,128)} %refs_7_.1, f32[1536,512]{1,0:T(8,128)} %refs_7_.1, f32[1536,512]{1,0:T(8,128)} %refs_7_.1, ...), custom_call_target="tpu_custom_call" | custom-call | flops 2415919104 | bytes 6291456 | tf_op jit(solution)/shard_map/pallas_call | solution.py:170
  107.2 1.8 %all-to-all-done.4 = f32[8,24,128]{2,1,0:T(8,128)S(1)} async-done(((f32[8,24,128]{2,1,0:T(8,128)}), f32[8,24,128]{2,1,0:T(8,128)S(1)}, u32[]{:S(2)}, u32[]{:S(2)}) %all-to-all-start.4) | async-done | bytes 98336 | tf_op jit(solution)/shard_map/all_to_all | solution.py:336
  109.0 5.7 %all-to-all-start.5 = ((f32[64,8,512]{2,1,0:T(8,128)}), f32[64,8,512]{2,1,0:T(8,128)S(1)}, u32[]{:S(2)}, u32[]{:S(2)}) async-start(f32[64,8,512]{2,1,0:T(8,128)} %bitcast.6), calls=%async_computation.5 | async-start | bytes 2097152 | tf_op jit(solution)/shard_map/all_to_all | solution.py:336
  114.8 2.2 %collective-permute-start.5 = (f32[160,128]{1,0:T(8,128)S(1)}, f32[160,128]{1,0:T(8,128)S(1)}, u32[]{:S(2)}, u32[]{:S(2)}) collective-permute-start(f32[160,128]{1,0:T(8,128)S(1)} %slice.36.refs_0_), channel_id=1, source_target_pairs={{0,2},{2,4},{4,6},{6,0},{1,3},{3,5},{5,7},{7,1},{8,10},{10,12},{12... | collective-permute-start | bytes 245768 | tf_op jit(solution)/shard_map/ppermute | solution.py:346
  117.0 2.5 %collective-permute-start.6 = (f32[160,128]{1,0:T(8,128)S(1)}, f32[160,128]{1,0:T(8,128)S(1)}, u32[]{:S(2)}, u32[]{:S(2)}) collective-permute-start(f32[160,128]{1,0:T(8,128)S(1)} %slice.36.refs_0_), channel_id=1, source_target_pairs={{0,4},{2,6},{4,0},{6,2},{1,5},{3,7},{5,1},{7,3},{8,12},{10,14},{12... | collective-permute-start | bytes 245768 | tf_op jit(solution)/shard_map/ppermute | solution.py:346
  119.5 3.7 %collective-permute-start.7 = (f32[160,128]{1,0:T(8,128)S(1)}, f32[160,128]{1,0:T(8,128)S(1)}, u32[]{:S(2)}, u32[]{:S(2)}) collective-permute-start(f32[160,128]{1,0:T(8,128)S(1)} %slice.36.refs_0_), channel_id=1, source_target_pairs={{0,6},{2,0},{4,2},{6,4},{1,7},{3,1},{5,3},{7,5},{8,14},{10,8},{12,... | collective-permute-start | bytes 245768 | tf_op jit(solution)/shard_map/ppermute | solution.py:346
  123.2 0.7 collective-permute-done.6.refs_2_
  124.0 2.2 %collective-permute-done.7.refs_3_ = f32[160,128]{1,0:T(8,128)S(1)} collective-permute-done((f32[160,128]{1,0:T(8,128)S(1)}, f32[160,128]{1,0:T(8,128)S(1)}, u32[]{:S(2)}, u32[]{:S(2)}) %collective-permute-start.7) | collective-permute-done | bytes 81952 | tf_op jit(solution)/shard_map/ppermute | solution.py:346
  126.2 3.5 %collective-permute-start.8 = (f32[640,128]{1,0:T(8,128)S(1)}, f32[640,128]{1,0:T(8,128)S(1)}, u32[]{:S(2)}, u32[]{:S(2)}) collective-permute-start(f32[640,128]{1,0:T(8,128)S(1)} %pad_maximum_fusion.1), channel_id=1, source_target_pairs={{0,1},{1,0},{2,3},{3,2},{4,5},{5,4},{6,7},{7,6},{8,9},{9,8},{10,11... | collective-permute-start | bytes 983048 | tf_op jit(solution)/shard_map/ppermute | solution.py:346
  129.7 1.1 collective-permute-done.8
  130.8 15.6 %shard_map.44 = (f32[512,512]{1,0:T(8,128)S(1)}, f32[192,512]{1,0:T(8,128)}) custom-call(s32[2]{0:T(128)S(1)} %pad_add_fusion.place_ref, f32[192,512]{1,0:T(8,128)S(1)} %reduce_sum.45.images_ref.refs_8_, f32[160,128]{1,0:T(8,128)S(1)} %slice.36.refs_0_, f32[160,128]{1,0:T(8,128)S(1)} %collective-permute-done.5.refs_1_, ...), custom_call_target="tpu_custom_call" | custom-call | flops 524288 | bytes 512 | tf_op jit(solution)/shard_map/pallas_call | solution.py:311
  146.5 1.6 %fusion.2 = f32[8,512]{1,0:T(8,128)} fusion(f32[8,512]{1,0:T(8,128)S(1)} %reduce_sum.49, f32[512,512]{1,0:T(8,128)S(1)} %get-tuple-element.19), kind=kOutput, calls=%fused_computation.5 | convolution fusion | flops 25165824 | bytes 1081344 | tf_op jit(solution)/shard_map/dot_general | solution.py:23
  (23 shorter events, 1.6 us)
Async XLA Ops:
  0.7 1.9 %copy-start = (f32[1536,512]{1,0:T(8,128)S(1)}, f32[1536,512]{1,0:T(8,128)}, u32[]{:S(2)}) copy-start(f32[1536,512]{1,0:T(8,128)} %refs_7_.1) | copy-start | bytes 9437188
  2.6 1.2 copy-start.1
  6.2 11.8 %collective-permute-start = (f32[768,512]{1,0:T(8,128)S(1)}, f32[768,512]{1,0:T(8,128)S(1)}, u32[]{:S(2)}, u32[]{:S(2)}) collective-permute-start(f32[768,512]{1,0:T(8,128)S(1)} %shard_map.42), channel_id=1, source_target_pairs={{0,1},{1,0},{2,3},{3,2},{4,5},{5,4},{6,7},{7,6},{8,9},{9,8},{10,11... | collective-permute-start | bytes 4718600 | tf_op jit(solution)/shard_map/ppermute | solution.py:346
  42.4 4.4 %collective-permute-start.1 = (f32[640,128]{1,0:T(8,128)S(1)}, f32[640,128]{1,0:T(8,128)S(1)}, u32[]{:S(2)}, u32[]{:S(2)}) collective-permute-start(f32[640,128]{1,0:T(8,128)S(1)} %get-tuple-element.12), channel_id=1, source_target_pairs={{0,1},{1,0},{2,3},{3,2},{4,5},{5,4},{6,7},{7,6},{8,9},{9,8},{10,11... | collective-permute-start | bytes 983048 | tf_op jit(solution)/shard_map/ppermute | solution.py:346
  47.6 14.2 %all-to-all-start.1 = ((f32[4,160,128]{2,1,0:T(8,128)}), f32[4,160,128]{2,1,0:T(8,128)S(1)}, u32[]{:S(2)}, u32[]{:S(2)}) async-start(f32[4,160,128]{2,1,0:T(8,128)} %bitcast.3), calls=%async_computation.1 | async-start | bytes 655360 | tf_op jit(solution)/shard_map/all_to_all | solution.py:336
  51.0 38.6 %collective-permute-start.2 = (f32[192,512]{1,0:T(8,128)S(1)}, f32[192,512]{1,0:T(8,128)S(1)}, u32[]{:S(2)}, u32[]{:S(2)}) collective-permute-start(f32[192,512]{1,0:T(8,128)S(1)} %reduce_sum.45.images_ref.refs_8_), channel_id=1, source_target_pairs={{0,2},{2,4},{4,6},{6,0},{1,3},{3,5},{5,7},{7,1},{8,10},{10,12},{12... | collective-permute-start | bytes 1179656 | tf_op jit(solution)/shard_map/ppermute | solution.py:346
  54.3 35.3 %collective-permute-start.3 = (f32[192,512]{1,0:T(8,128)S(1)}, f32[192,512]{1,0:T(8,128)S(1)}, u32[]{:S(2)}, u32[]{:S(2)}) collective-permute-start(f32[192,512]{1,0:T(8,128)S(1)} %reduce_sum.45.images_ref.refs_8_), channel_id=1, source_target_pairs={{0,4},{2,6},{4,0},{6,2},{1,5},{3,7},{5,1},{7,3},{8,12},{10,14},{12... | collective-permute-start | bytes 1179656 | tf_op jit(solution)/shard_map/ppermute | solution.py:346
  58.7 31.0 %collective-permute-start.4 = (f32[192,512]{1,0:T(8,128)S(1)}, f32[192,512]{1,0:T(8,128)S(1)}, u32[]{:S(2)}, u32[]{:S(2)}) collective-permute-start(f32[192,512]{1,0:T(8,128)S(1)} %reduce_sum.45.images_ref.refs_8_), channel_id=1, source_target_pairs={{0,6},{2,0},{4,2},{6,4},{1,7},{3,1},{5,3},{7,5},{8,14},{10,8},{12,... | collective-permute-start | bytes 1179656 | tf_op jit(solution)/shard_map/ppermute | solution.py:346
  90.9 10.1 %collective-permute-start.9 = (f32[768,512]{1,0:T(8,128)}, f32[768,512]{1,0:T(8,128)S(1)}, u32[]{:S(2)}, u32[]{:S(2)}) collective-permute-start(f32[768,512]{1,0:T(8,128)} %pad_maximum_fusion), channel_id=1, source_target_pairs={{0,1},{1,0},{2,3},{3,2},{4,5},{5,4},{6,7},{7,6},{8,9},{9,8},{10,11... | collective-permute-start | bytes 4718600 | tf_op jit(solution)/shard_map/ppermute | solution.py:346
  97.7 11.4 %all-to-all-start.4 = ((f32[8,24,128]{2,1,0:T(8,128)}), f32[8,24,128]{2,1,0:T(8,128)S(1)}, u32[]{:S(2)}, u32[]{:S(2)}) async-start(f32[8,24,128]{2,1,0:T(8,128)} %broadcast_in_dim.5), calls=%async_computation.4 | async-start | bytes 196608 | tf_op jit(solution)/shard_map/all_to_all | solution.py:336
  109.0 37.4 %all-to-all-start.5 = ((f32[64,8,512]{2,1,0:T(8,128)}), f32[64,8,512]{2,1,0:T(8,128)S(1)}, u32[]{:S(2)}, u32[]{:S(2)}) async-start(f32[64,8,512]{2,1,0:T(8,128)} %bitcast.6), calls=%async_computation.5 | async-start | bytes 2097152 | tf_op jit(solution)/shard_map/all_to_all | solution.py:336
  114.8 8.4 %collective-permute-start.5 = (f32[160,128]{1,0:T(8,128)S(1)}, f32[160,128]{1,0:T(8,128)S(1)}, u32[]{:S(2)}, u32[]{:S(2)}) collective-permute-start(f32[160,128]{1,0:T(8,128)S(1)} %slice.36.refs_0_), channel_id=1, source_target_pairs={{0,2},{2,4},{4,6},{6,0},{1,3},{3,5},{5,7},{7,1},{8,10},{10,12},{12... | collective-permute-start | bytes 245768 | tf_op jit(solution)/shard_map/ppermute | solution.py:346
  117.0 7.0 %collective-permute-start.6 = (f32[160,128]{1,0:T(8,128)S(1)}, f32[160,128]{1,0:T(8,128)S(1)}, u32[]{:S(2)}, u32[]{:S(2)}) collective-permute-start(f32[160,128]{1,0:T(8,128)S(1)} %slice.36.refs_0_), channel_id=1, source_target_pairs={{0,4},{2,6},{4,0},{6,2},{1,5},{3,7},{5,1},{7,3},{8,12},{10,14},{12... | collective-permute-start | bytes 245768 | tf_op jit(solution)/shard_map/ppermute | solution.py:346
  119.5 6.6 %collective-permute-start.7 = (f32[160,128]{1,0:T(8,128)S(1)}, f32[160,128]{1,0:T(8,128)S(1)}, u32[]{:S(2)}, u32[]{:S(2)}) collective-permute-start(f32[160,128]{1,0:T(8,128)S(1)} %slice.36.refs_0_), channel_id=1, source_target_pairs={{0,6},{2,0},{4,2},{6,4},{1,7},{3,1},{5,3},{7,5},{8,14},{10,8},{12,... | collective-permute-start | bytes 245768 | tf_op jit(solution)/shard_map/ppermute | solution.py:346
  126.2 4.6 %collective-permute-start.8 = (f32[640,128]{1,0:T(8,128)S(1)}, f32[640,128]{1,0:T(8,128)S(1)}, u32[]{:S(2)}, u32[]{:S(2)}) collective-permute-start(f32[640,128]{1,0:T(8,128)S(1)} %pad_maximum_fusion.1), channel_id=1, source_target_pairs={{0,1},{1,0},{2,3},{3,2},{4,5},{5,4},{6,7},{7,6},{8,9},{9,8},{10,11... | collective-permute-start | bytes 983048 | tf_op jit(solution)/shard_map/ppermute | solution.py:346

commit v6 on v5

--- a/solution.py
+++ b/solution.py
@@ -15,13 +15,12 @@
 AHEAD = 2
 F32 = jnp.float32
 BF16 = jnp.bfloat16
-HIGHEST = lax.Precision.HIGHEST
 VMEM = 48 * 2**20
 
 
-def exact_dot(a, b, contract):
+def last_dot(a, b, contract):
     return lax.dot_general(
-        a, b, (contract, ((), ())), precision=HIGHEST, preferred_element_type=F32
+        a, b, (contract, ((), ())), precision=lax.Precision.HIGH, preferred_element_type=F32
     )
 
 
@@ -302,7 +301,9 @@
             work_ref[end:, end:] = work_ref[end:, end:] - change[:, end:]
             inverse_ref[first:end, end:] = jnp.zeros((BLOCK, size - end), F32)
         inverse_ref[first:end, :end] = finished
-        basis_ref[:, first:end] = scale * six_pass_dot(images_ref[:, :end], finished, 1, 1)
+        basis_ref[:, first:end] = scale * three_pass_dot(
+            [halves(images_ref[:, :end])], [halves(finished)], 1, 1
+        )
 
 
 def factor(pieces, images, place, scale):
@@ -383,7 +384,7 @@
     there = shifted(jnp.concatenate(here, 0), "core", 1)
     there = [there[s * slab_rows : (s + 1) * slab_rows] for s in range(groups)]
     inverse, basis = factor(here + there, own, place, scale)
-    return basis, exact_dot(moved.sum(0), inverse, ((1,), (1,)))
+    return basis, last_dot(moved.sum(0), inverse, ((1,), (1,)))
 
 
 def solution(mesh):

time: 149 us -> 148 us (level)
  no operation moved by 1% of the time
where the time goes in v6:
time: 148 us; the launch traced here: 147 us
  starting transfers between devices  53.2 us (36%)
  blocking collectives  50.7 us (34%)
  Pallas kernels  27 us (18%)
  waiting for transfers between devices  7.73 us (5%)
  local copies, waits for them, and re-layouts  3.93 us (3%)
  other arithmetic  2.79 us (2%)
    all_to_all x3, blocking collectives, exchange(): return lax.all_to_all(blocks, axes, 0, 0, tiled=True)  50.7 us
    ppermute x10, starting transfers between devices, shifted(): lax.ppermute(block, axis, [(i, (i + by) % size) for i in range(size)])  40.7 us
    pallas_call x1, Pallas kernels, factor(): pl.pallas_call(functools.partial(factor_kernel, scale, len(pieces) // COR...  15.3 us
    all_to_all x3, starting transfers between devices, exchange(): return lax.all_to_all(blocks, axes, 0, 0, tiled=True)  12.6 us
    pallas_call x1, Pallas kernels, moved_rows(): pl.pallas_call(functools.partial(moved_kernel, len(images)), grid_spec=pl...  6.02 us
    ppermute x10, waiting for transfers between devices, shifted(): lax.ppermute(block, axis, [(i, (i + by) % size) for i in range(size)])  5.9 us
    pallas_call x2, Pallas kernels, partial_images(): pl.pallas_call(images_kernel, grid_spec=pltpu.PrefetchScalarGridSpec(num_...  4.66 us
    unnamed x4, local copies, waits for them, and re-layouts  3.11 us
  transfers between devices with their start and end apart: 13, of which 6 were waited for; matrix products, arithmetic and copies ran while one was open for 1% of the time, Pallas kernels for 16%

profile of v6, /device:TPU:1, one launch (start us, length us, event | category | flops | bytes accessed | tf_op | source)
XLA Modules:
  0.0 147.3 jit_solution(16799067085488306839)
XLA Ops:
  0.7 1.9 %copy-done = f32[1536,512]{1,0:T(8,128)S(1)} copy-done((f32[1536,512]{1,0:T(8,128)S(1)}, f32[1536,512]{1,0:T(8,128)}, u32[]{:S(2)}) %copy-start) | copy-done | bytes 3145752
  2.6 1.2 copy-done.1
  3.8 2.3 %shard_map.42 = f32[768,512]{1,0:T(8,128)S(1)} custom-call(s32[2]{0:T(128)S(1)} %pad_add_fusion.place_ref, f32[1536,512]{1,0:T(8,128)S(1)} %copy-done, f32[1536,512]{1,0:T(8,128)S(1)} %copy-done, f32[512,512]{1,0:T(8,128)S(1)} %copy-done.1), custom_call_target="tpu_custom_call" | custom-call | flops 1207959552 | bytes 6291456 | tf_op jit(solution)/shard_map/pallas_call | solution.py:81
  6.2 8.8 %collective-permute-start = (f32[768,512]{1,0:T(8,128)S(1)}, f32[768,512]{1,0:T(8,128)S(1)}, u32[]{:S(2)}, u32[]{:S(2)}) collective-permute-start(f32[768,512]{1,0:T(8,128)S(1)} %shard_map.42), channel_id=1, source_target_pairs={{0,1},{1,0},{2,3},{3,2},{4,5},{5,4},{6,7},{7,6},{8,9},{9,8},{10,11... | collective-permute-start | bytes 4718600 | tf_op jit(solution)/shard_map/ppermute | solution.py:347
  15.0 2.3 %shard_map.41 = f32[768,512]{1,0:T(8,128)S(1)} custom-call(s32[2]{0:T(128)S(1)} %pad_add_fusion.place_ref, f32[1536,512]{1,0:T(8,128)S(1)} %copy-done, f32[1536,512]{1,0:T(8,128)S(1)} %copy-done, f32[512,512]{1,0:T(8,128)S(1)} %copy-done.1), custom_call_target="tpu_custom_call" | custom-call | flops 1207959552 | bytes 6291456 | tf_op jit(solution)/shard_map/pallas_call | solution.py:81
  17.3 0.7 collective-permute-done
  18.3 22.9 %all_to_all.30 = f32[4,192,512]{2,1,0:T(8,128)S(1)} all-to-all(f32[4,192,512]{2,1,0:T(8,128)S(1)} %bitcast.9), channel_id=1, replica_groups=mesh['z'=8,'y'=8,'x'=4,'core'=2] {'x'}, dimensions={0} | all-to-all | bytes 3145728 | tf_op jit(solution)/shard_map/all_to_all | solution.py:337
  41.4 1.0 shard_map.43
  42.4 3.1 %collective-permute-start.1 = (f32[640,128]{1,0:T(8,128)S(1)}, f32[640,128]{1,0:T(8,128)S(1)}, u32[]{:S(2)}, u32[]{:S(2)}) collective-permute-start(f32[640,128]{1,0:T(8,128)S(1)} %get-tuple-element.12), channel_id=1, source_target_pairs={{0,1},{1,0},{2,3},{3,2},{4,5},{5,4},{6,7},{7,6},{8,9},{9,8},{10,11... | collective-permute-start | bytes 983048 | tf_op jit(solution)/shard_map/ppermute | solution.py:347
  45.6 1.2 collective-permute-done.1
  46.8 0.8 add.9
  47.6 3.5 %all-to-all-start.1 = ((f32[4,160,128]{2,1,0:T(8,128)}), f32[4,160,128]{2,1,0:T(8,128)S(1)}, u32[]{:S(2)}, u32[]{:S(2)}) async-start(f32[4,160,128]{2,1,0:T(8,128)} %bitcast.3), calls=%async_computation.1 | async-start | bytes 655360 | tf_op jit(solution)/shard_map/all_to_all | solution.py:337
  51.0 3.3 %collective-permute-start.2 = (f32[192,512]{1,0:T(8,128)S(1)}, f32[192,512]{1,0:T(8,128)S(1)}, u32[]{:S(2)}, u32[]{:S(2)}) collective-permute-start(f32[192,512]{1,0:T(8,128)S(1)} %reduce_sum.45.images_ref.refs_8_), channel_id=1, source_target_pairs={{0,2},{2,4},{4,6},{6,0},{1,3},{3,5},{5,7},{7,1},{8,10},{10,12},{12... | collective-permute-start | bytes 1179656 | tf_op jit(solution)/shard_map/ppermute | solution.py:347
  54.3 4.3 %collective-permute-start.3 = (f32[192,512]{1,0:T(8,128)S(1)}, f32[192,512]{1,0:T(8,128)S(1)}, u32[]{:S(2)}, u32[]{:S(2)}) collective-permute-start(f32[192,512]{1,0:T(8,128)S(1)} %reduce_sum.45.images_ref.refs_8_), channel_id=1, source_target_pairs={{0,4},{2,6},{4,0},{6,2},{1,5},{3,7},{5,1},{7,3},{8,12},{10,14},{12... | collective-permute-start | bytes 1179656 | tf_op jit(solution)/shard_map/ppermute | solution.py:347
  58.7 3.1 %collective-permute-start.4 = (f32[192,512]{1,0:T(8,128)S(1)}, f32[192,512]{1,0:T(8,128)S(1)}, u32[]{:S(2)}, u32[]{:S(2)}) collective-permute-start(f32[192,512]{1,0:T(8,128)S(1)} %reduce_sum.45.images_ref.refs_8_), channel_id=1, source_target_pairs={{0,6},{2,0},{4,2},{6,4},{1,7},{3,1},{5,3},{7,5},{8,14},{10,8},{12,... | collective-permute-start | bytes 1179656 | tf_op jit(solution)/shard_map/ppermute | solution.py:347
  61.8 10.2 %all_to_all.31 = f32[8,24,128]{2,1,0:T(8,128)S(1)} all-to-all(f32[8,24,128]{2,1,0:T(8,128)S(1)} %bitcast.10), channel_id=1, replica_groups=mesh['z'=8,'y'=8,'x'=4,'core'=2] {'y'}, dimensions={0} | all-to-all | bytes 196608 | tf_op jit(solution)/shard_map/all_to_all | solution.py:337
  72.1 17.5 %all_to_all.32 = f32[8,24,128]{2,1,0:T(8,128)S(1)} all-to-all(f32[8,24,128]{2,1,0:T(8,128)S(1)} %broadcast_in_dim.4), channel_id=1, replica_groups=mesh['z'=8,'y'=8,'x'=4,'core'=2] {'z'}, dimensions={0} | all-to-all | bytes 196608 | tf_op jit(solution)/shard_map/all_to_all | solution.py:337
  89.6 1.3 pad_maximum_fusion
  90.9 6.1 %collective-permute-start.9 = (f32[768,512]{1,0:T(8,128)}, f32[768,512]{1,0:T(8,128)S(1)}, u32[]{:S(2)}, u32[]{:S(2)}) collective-permute-start(f32[768,512]{1,0:T(8,128)} %pad_maximum_fusion), channel_id=1, source_target_pairs={{0,1},{1,0},{2,3},{3,2},{4,5},{5,4},{6,7},{7,6},{8,9},{9,8},{10,11... | collective-permute-start | bytes 4718600 | tf_op jit(solution)/shard_map/ppermute | solution.py:347
  97.7 3.4 %all-to-all-start.4 = ((f32[8,24,128]{2,1,0:T(8,128)}), f32[8,24,128]{2,1,0:T(8,128)S(1)}, u32[]{:S(2)}, u32[]{:S(2)}) async-start(f32[8,24,128]{2,1,0:T(8,128)} %broadcast_in_dim.5), calls=%async_computation.4 | async-start | bytes 196608 | tf_op jit(solution)/shard_map/all_to_all | solution.py:337
  101.2 6.0 %shard_map.45 = f32[512,512]{1,0:T(8,128)} custom-call(s32[2]{0:T(128)S(1)} %pad_add_fusion.place_ref, f32[1536,512]{1,0:T(8,128)} %refs_7_.1, f32[1536,512]{1,0:T(8,128)} %refs_7_.1, f32[1536,512]{1,0:T(8,128)} %refs_7_.1, f32[1536,512]{1,0:T(8,128)} %refs_7_.1, f32[1536,512]{1,0:T(8,128)} %refs_7_.1, f32[1536,512]{1,0:T(8,128)} %refs_7_.1, ...), custom_call_target="tpu_custom_call" | custom-call | flops 2415919104 | bytes 6291456 | tf_op jit(solution)/shard_map/pallas_call | solution.py:169
  107.2 1.8 %all-to-all-done.4 = f32[8,24,128]{2,1,0:T(8,128)S(1)} async-done(((f32[8,24,128]{2,1,0:T(8,128)}), f32[8,24,128]{2,1,0:T(8,128)S(1)}, u32[]{:S(2)}, u32[]{:S(2)}) %all-to-all-start.4) | async-done | bytes 98336 | tf_op jit(solution)/shard_map/all_to_all | solution.py:337
  109.0 5.7 %all-to-all-start.5 = ((f32[64,8,512]{2,1,0:T(8,128)}), f32[64,8,512]{2,1,0:T(8,128)S(1)}, u32[]{:S(2)}, u32[]{:S(2)}) async-start(f32[64,8,512]{2,1,0:T(8,128)} %bitcast.6), calls=%async_computation.5 | async-start | bytes 2097152 | tf_op jit(solution)/shard_map/all_to_all | solution.py:337
  114.8 2.2 %collective-permute-start.5 = (f32[160,128]{1,0:T(8,128)S(1)}, f32[160,128]{1,0:T(8,128)S(1)}, u32[]{:S(2)}, u32[]{:S(2)}) collective-permute-start(f32[160,128]{1,0:T(8,128)S(1)} %slice.36.refs_0_), channel_id=1, source_target_pairs={{0,2},{2,4},{4,6},{6,0},{1,3},{3,5},{5,7},{7,1},{8,10},{10,12},{12... | collective-permute-start | bytes 245768 | tf_op jit(solution)/shard_map/ppermute | solution.py:347
  117.0 2.5 %collective-permute-start.6 = (f32[160,128]{1,0:T(8,128)S(1)}, f32[160,128]{1,0:T(8,128)S(1)}, u32[]{:S(2)}, u32[]{:S(2)}) collective-permute-start(f32[160,128]{1,0:T(8,128)S(1)} %slice.36.refs_0_), channel_id=1, source_target_pairs={{0,4},{2,6},{4,0},{6,2},{1,5},{3,7},{5,1},{7,3},{8,12},{10,14},{12... | collective-permute-start | bytes 245768 | tf_op jit(solution)/shard_map/ppermute | solution.py:347
  119.5 3.7 %collective-permute-start.7 = (f32[160,128]{1,0:T(8,128)S(1)}, f32[160,128]{1,0:T(8,128)S(1)}, u32[]{:S(2)}, u32[]{:S(2)}) collective-permute-start(f32[160,128]{1,0:T(8,128)S(1)} %slice.36.refs_0_), channel_id=1, source_target_pairs={{0,6},{2,0},{4,2},{6,4},{1,7},{3,1},{5,3},{7,5},{8,14},{10,8},{12,... | collective-permute-start | bytes 245768 | tf_op jit(solution)/shard_map/ppermute | solution.py:347
  123.2 0.7 collective-permute-done.6.refs_2_
  124.0 2.2 %collective-permute-done.7.refs_3_ = f32[160,128]{1,0:T(8,128)S(1)} collective-permute-done((f32[160,128]{1,0:T(8,128)S(1)}, f32[160,128]{1,0:T(8,128)S(1)}, u32[]{:S(2)}, u32[]{:S(2)}) %collective-permute-start.7) | collective-permute-done | bytes 81952 | tf_op jit(solution)/shard_map/ppermute | solution.py:347
  126.2 3.5 %collective-permute-start.8 = (f32[640,128]{1,0:T(8,128)S(1)}, f32[640,128]{1,0:T(8,128)S(1)}, u32[]{:S(2)}, u32[]{:S(2)}) collective-permute-start(f32[640,128]{1,0:T(8,128)S(1)} %pad_maximum_fusion.1), channel_id=1, source_target_pairs={{0,1},{1,0},{2,3},{3,2},{4,5},{5,4},{6,7},{7,6},{8,9},{9,8},{10,11... | collective-permute-start | bytes 983048 | tf_op jit(solution)/shard_map/ppermute | solution.py:347
  129.7 1.1 collective-permute-done.8
  130.8 15.3 %shard_map.44 = (f32[512,512]{1,0:T(8,128)S(1)}, f32[192,512]{1,0:T(8,128)}) custom-call(s32[2]{0:T(128)S(1)} %pad_add_fusion.place_ref, f32[192,512]{1,0:T(8,128)S(1)} %reduce_sum.45.images_ref.refs_8_, f32[160,128]{1,0:T(8,128)S(1)} %slice.36.refs_0_, f32[160,128]{1,0:T(8,128)S(1)} %collective-permute-done.5.refs_1_, ...), custom_call_target="tpu_custom_call" | custom-call | flops 524288 | bytes 512 | tf_op jit(solution)/shard_map/pallas_call | solution.py:312
  146.2 1.1 fusion.2
  (23 shorter events, 1.6 us)
Async XLA Ops:
  0.7 1.9 %copy-start = (f32[1536,512]{1,0:T(8,128)S(1)}, f32[1536,512]{1,0:T(8,128)}, u32[]{:S(2)}) copy-start(f32[1536,512]{1,0:T(8,128)} %refs_7_.1) | copy-start | bytes 9437188
  2.6 1.2 copy-start.1
  6.2 11.8 %collective-permute-start = (f32[768,512]{1,0:T(8,128)S(1)}, f32[768,512]{1,0:T(8,128)S(1)}, u32[]{:S(2)}, u32[]{:S(2)}) collective-permute-start(f32[768,512]{1,0:T(8,128)S(1)} %shard_map.42), channel_id=1, source_target_pairs={{0,1},{1,0},{2,3},{3,2},{4,5},{5,4},{6,7},{7,6},{8,9},{9,8},{10,11... | collective-permute-start | bytes 4718600 | tf_op jit(solution)/shard_map/ppermute | solution.py:347
  42.4 4.4 %collective-permute-start.1 = (f32[640,128]{1,0:T(8,128)S(1)}, f32[640,128]{1,0:T(8,128)S(1)}, u32[]{:S(2)}, u32[]{:S(2)}) collective-permute-start(f32[640,128]{1,0:T(8,128)S(1)} %get-tuple-element.12), channel_id=1, source_target_pairs={{0,1},{1,0},{2,3},{3,2},{4,5},{5,4},{6,7},{7,6},{8,9},{9,8},{10,11... | collective-permute-start | bytes 983048 | tf_op jit(solution)/shard_map/ppermute | solution.py:347
  47.6 14.2 %all-to-all-start.1 = ((f32[4,160,128]{2,1,0:T(8,128)}), f32[4,160,128]{2,1,0:T(8,128)S(1)}, u32[]{:S(2)}, u32[]{:S(2)}) async-start(f32[4,160,128]{2,1,0:T(8,128)} %bitcast.3), calls=%async_computation.1 | async-start | bytes 655360 | tf_op jit(solution)/shard_map/all_to_all | solution.py:337
  51.0 38.6 %collective-permute-start.2 = (f32[192,512]{1,0:T(8,128)S(1)}, f32[192,512]{1,0:T(8,128)S(1)}, u32[]{:S(2)}, u32[]{:S(2)}) collective-permute-start(f32[192,512]{1,0:T(8,128)S(1)} %reduce_sum.45.images_ref.refs_8_), channel_id=1, source_target_pairs={{0,2},{2,4},{4,6},{6,0},{1,3},{3,5},{5,7},{7,1},{8,10},{10,12},{12... | collective-permute-start | bytes 1179656 | tf_op jit(solution)/shard_map/ppermute | solution.py:347
  54.3 35.3 %collective-permute-start.3 = (f32[192,512]{1,0:T(8,128)S(1)}, f32[192,512]{1,0:T(8,128)S(1)}, u32[]{:S(2)}, u32[]{:S(2)}) collective-permute-start(f32[192,512]{1,0:T(8,128)S(1)} %reduce_sum.45.images_ref.refs_8_), channel_id=1, source_target_pairs={{0,4},{2,6},{4,0},{6,2},{1,5},{3,7},{5,1},{7,3},{8,12},{10,14},{12... | collective-permute-start | bytes 1179656 | tf_op jit(solution)/shard_map/ppermute | solution.py:347
  58.7 31.0 %collective-permute-start.4 = (f32[192,512]{1,0:T(8,128)S(1)}, f32[192,512]{1,0:T(8,128)S(1)}, u32[]{:S(2)}, u32[]{:S(2)}) collective-permute-start(f32[192,512]{1,0:T(8,128)S(1)} %reduce_sum.45.images_ref.refs_8_), channel_id=1, source_target_pairs={{0,6},{2,0},{4,2},{6,4},{1,7},{3,1},{5,3},{7,5},{8,14},{10,8},{12,... | collective-permute-start | bytes 1179656 | tf_op jit(solution)/shard_map/ppermute | solution.py:347
  90.9 10.1 %collective-permute-start.9 = (f32[768,512]{1,0:T(8,128)}, f32[768,512]{1,0:T(8,128)S(1)}, u32[]{:S(2)}, u32[]{:S(2)}) collective-permute-start(f32[768,512]{1,0:T(8,128)} %pad_maximum_fusion), channel_id=1, source_target_pairs={{0,1},{1,0},{2,3},{3,2},{4,5},{5,4},{6,7},{7,6},{8,9},{9,8},{10,11... | collective-permute-start | bytes 4718600 | tf_op jit(solution)/shard_map/ppermute | solution.py:347
  97.7 11.4 %all-to-all-start.4 = ((f32[8,24,128]{2,1,0:T(8,128)}), f32[8,24,128]{2,1,0:T(8,128)S(1)}, u32[]{:S(2)}, u32[]{:S(2)}) async-start(f32[8,24,128]{2,1,0:T(8,128)} %broadcast_in_dim.5), calls=%async_computation.4 | async-start | bytes 196608 | tf_op jit(solution)/shard_map/all_to_all | solution.py:337
  109.0 37.1 %all-to-all-start.5 = ((f32[64,8,512]{2,1,0:T(8,128)}), f32[64,8,512]{2,1,0:T(8,128)S(1)}, u32[]{:S(2)}, u32[]{:S(2)}) async-start(f32[64,8,512]{2,1,0:T(8,128)} %bitcast.6), calls=%async_computation.5 | async-start | bytes 2097152 | tf_op jit(solution)/shard_map/all_to_all | solution.py:337
  114.8 8.4 %collective-permute-start.5 = (f32[160,128]{1,0:T(8,128)S(1)}, f32[160,128]{1,0:T(8,128)S(1)}, u32[]{:S(2)}, u32[]{:S(2)}) collective-permute-start(f32[160,128]{1,0:T(8,128)S(1)} %slice.36.refs_0_), channel_id=1, source_target_pairs={{0,2},{2,4},{4,6},{6,0},{1,3},{3,5},{5,7},{7,1},{8,10},{10,12},{12... | collective-permute-start | bytes 245768 | tf_op jit(solution)/shard_map/ppermute | solution.py:347
  117.0 7.0 %collective-permute-start.6 = (f32[160,128]{1,0:T(8,128)S(1)}, f32[160,128]{1,0:T(8,128)S(1)}, u32[]{:S(2)}, u32[]{:S(2)}) collective-permute-start(f32[160,128]{1,0:T(8,128)S(1)} %slice.36.refs_0_), channel_id=1, source_target_pairs={{0,4},{2,6},{4,0},{6,2},{1,5},{3,7},{5,1},{7,3},{8,12},{10,14},{12... | collective-permute-start | bytes 245768 | tf_op jit(solution)/shard_map/ppermute | solution.py:347
  119.5 6.6 %collective-permute-start.7 = (f32[160,128]{1,0:T(8,128)S(1)}, f32[160,128]{1,0:T(8,128)S(1)}, u32[]{:S(2)}, u32[]{:S(2)}) collective-permute-start(f32[160,128]{1,0:T(8,128)S(1)} %slice.36.refs_0_), channel_id=1, source_target_pairs={{0,6},{2,0},{4,2},{6,4},{1,7},{3,1},{5,3},{7,5},{8,14},{10,8},{12,... | collective-permute-start | bytes 245768 | tf_op jit(solution)/shard_map/ppermute | solution.py:347
  126.2 4.6 %collective-permute-start.8 = (f32[640,128]{1,0:T(8,128)S(1)}, f32[640,128]{1,0:T(8,128)S(1)}, u32[]{:S(2)}, u32[]{:S(2)}) collective-permute-start(f32[640,128]{1,0:T(8,128)S(1)} %pad_maximum_fusion.1), channel_id=1, source_target_pairs={{0,1},{1,0},{2,3},{3,2},{4,5},{5,4},{6,7},{7,6},{8,9},{9,8},{10,11... | collective-permute-start | bytes 983048 | tf_op jit(solution)/shard_map/ppermute | solution.py:347
